TPU v7x, 256 devices: a whole 4x4x8 slice. The times are simulated.
256 devices in a mesh: rep: 16 (over x, y_hi, core), fsdp: 16 (over y_lo, z).
Axes of the slice: x: 4, y: 4 (y_hi: 2, y_lo: 2; y = y_hi * 2 + y_lo), z: 8, core: 2. Of those that a mesh axis runs over, the one named last changes fastest.
Arguments:
- activations: bfloat16 [65536, 4096], P(('rep', 'fsdp')), may hold values from -200 to 200
- queries: bfloat16 [65536, 4096], P(('rep', 'fsdp')), may hold values from -18 to 18
- attention_output_cotangent: bfloat16 [65536, 4096], P(('rep', 'fsdp')), may hold values from -4 to 4
- document_ids: int32 [256, 256], P(('rep', 'fsdp')), may hold values from 0 to 3, never falling along the last dimension, each value on 1 to 128 neighbouring positions
- norm_gain: bfloat16 [16, 4096], P('rep', 'fsdp'), may hold values from 0.5 to 1.5
- key_value_weight: bfloat16 [16, 4096, 1024], P('rep', 'fsdp'), may hold values from -0.09375 to 0.09375
- fragment_local: bfloat16 [16, 4096, 1024], P('rep', 'fsdp'), may hold values from -6 to 6
- fragment_master: float32 [4096, 1024], P('fsdp', 'rep'), may hold values from -6 to 6
- fragment_moment: float32 [4096, 1024], P('fsdp', 'rep'), may hold values from -6 to 6
Outputs:
- query_gradient: bfloat16 [65536, 4096], P(('rep', 'fsdp'))
- input_gradient: bfloat16 [65536, 4096], P(('rep', 'fsdp'))
- weight_gradient: float32 [16, 4096, 1024], P('rep', 'fsdp')
- gain_gradient: float32 [16, 4096], P('rep', 'fsdp')
- master_next: float32 [4096, 1024], P('fsdp', 'rep')
- moment_next: float32 [4096, 1024], P('fsdp', 'rep')
- fragment_next: bfloat16 [16, 4096, 1024], P('rep', 'fsdp')
Inputs may be any that keep to these rules, and one draw needn't show every extreme that they name: `document_ids`: along each row the numbers never fall; every number from 0 to 3 appears in every row, on at most 128 tokens.
All inputs are finite; a program needn't handle non-finite values.
Results may differ from a plain program's by a relative error of at most 0.023.
Values may be sent and summed in bfloat16 or wider, within the bound.
A program may use at most 128 MiB of HBM per device.

v0:
```python
import jax
import jax.numpy as jnp
from jax import lax
from jax.sharding import PartitionSpec as P

QUERY_HEADS = 32
KEY_VALUE_HEADS = 4
HEAD_DIMENSION = 128


epsilon = 1e-05
rope_base = 500000.0
outer_rate = 0.7
outer_momentum = 0.9
mixing = 0.5
masked_score = -1e30


def doc_positions(document_row):
    sequence_length = document_row.shape[0]
    index = jnp.arange(sequence_length, dtype=jnp.int32)
    changed = jnp.concatenate(
        [jnp.ones((1,), jnp.int32), (document_row[1:] != document_row[:-1]).astype(jnp.int32)]
    )
    first = lax.cummax(jnp.where(changed > 0, index, jnp.zeros_like(index)), axis=0)
    return index - first


def rope_tables(document_row):
    half = HEAD_DIMENSION // 2
    frequency = jnp.power(
        jnp.float32(rope_base), -2.0 * jnp.arange(half, dtype=jnp.float32) / HEAD_DIMENSION
    )
    angle = doc_positions(document_row).astype(jnp.float32)[:, None] * frequency[None, :]
    cosine = jnp.concatenate([jnp.cos(angle), jnp.cos(angle)], axis=1)
    sine = jnp.concatenate([jnp.sin(angle), jnp.sin(angle)], axis=1)
    return (cosine[:, None, :], sine[:, None, :])


def rotate(block):
    half = block.shape[-1] // 2
    return jnp.concatenate([-block[..., half:], block[..., :half]], axis=-1)


def rotate_back(block):
    half = block.shape[-1] // 2
    return jnp.concatenate([block[..., half:], -block[..., :half]], axis=-1)


def attention_terms(queries, attention_output_cotangent, keys, value_rows, document_row):
    sequence_length = queries.shape[0]
    query_group = QUERY_HEADS // KEY_VALUE_HEADS
    scale = HEAD_DIMENSION ** (-0.5)
    heads_of_query = queries.reshape(sequence_length, KEY_VALUE_HEADS, query_group, HEAD_DIMENSION)
    heads_cotangent = attention_output_cotangent.reshape(
        sequence_length, KEY_VALUE_HEADS, query_group, HEAD_DIMENSION
    )
    index = jnp.arange(sequence_length, dtype=jnp.int32)
    allowed = (index[None, :] <= index[:, None]) & (document_row[None, :] == document_row[:, None])
    scores = (
        jnp.einsum("tkgd,skd->kgts", heads_of_query, keys, preferred_element_type=jnp.float32)
        * scale
    )
    scores = jnp.where(allowed, scores, masked_score)
    highest = jnp.max(scores, axis=3, keepdims=True)
    exponent = jnp.exp(scores - highest)
    attention_weights = exponent / jnp.sum(exponent, axis=3, keepdims=True)
    weights_half = attention_weights.astype(jnp.bfloat16)
    weight_cotangent = jnp.einsum(
        "tkgd,skd->kgts", heads_cotangent, value_rows, preferred_element_type=jnp.float32
    )
    row_delta = jnp.sum(attention_weights * weight_cotangent, axis=3, keepdims=True)
    score_cotangent = (attention_weights * (weight_cotangent - row_delta) * scale).astype(
        jnp.bfloat16
    )
    query_gradient = jnp.einsum(
        "kgts,skd->tkgd", score_cotangent, keys, preferred_element_type=jnp.float32
    )
    query_gradient = query_gradient.astype(jnp.bfloat16).reshape(
        sequence_length, QUERY_HEADS * HEAD_DIMENSION
    )
    key_cotangent = jnp.einsum(
        "kgts,tkgd->skd", score_cotangent, heads_of_query, preferred_element_type=jnp.float32
    )
    cotangent_of_value = jnp.einsum(
        "kgts,tkgd->skd", weights_half, heads_cotangent, preferred_element_type=jnp.float32
    )
    return (query_gradient, key_cotangent, cotangent_of_value)


def inner_step(
    activations, queries, attention_output_cotangent, document_ids, norm_gain, key_value_weight
):
    sequence_length = activations.shape[0]
    wide = activations.astype(jnp.float32)
    inverse = lax.rsqrt(jnp.mean(wide * wide, axis=1, keepdims=True) + epsilon)
    gain_rows = norm_gain[0]
    weight_rows = key_value_weight[0]
    gain_piece = lax.all_gather(gain_rows, "fsdp", axis=0, tiled=True)
    weight_piece = lax.all_gather(weight_rows, "fsdp", axis=0, tiled=True)
    normed_piece = (wide * inverse * gain_piece.astype(jnp.float32)).astype(jnp.bfloat16)
    projected_rows = jnp.dot(normed_piece, weight_piece, preferred_element_type=jnp.float32)
    document_row = document_ids[0]
    cosine, sine = rope_tables(document_row)
    key_unprocessed = projected_rows[:, : KEY_VALUE_HEADS * HEAD_DIMENSION].reshape(
        sequence_length, KEY_VALUE_HEADS, HEAD_DIMENSION
    )
    keys = (key_unprocessed * cosine + rotate(key_unprocessed) * sine).astype(jnp.bfloat16)
    value_rows = (
        projected_rows[:, KEY_VALUE_HEADS * HEAD_DIMENSION :]
        .reshape(sequence_length, KEY_VALUE_HEADS, HEAD_DIMENSION)
        .astype(jnp.bfloat16)
    )
    query_gradient, key_cotangent, cotangent_of_value = attention_terms(
        queries, attention_output_cotangent, keys, value_rows, document_row
    )
    unrotated_key = key_cotangent * cosine + rotate_back(key_cotangent * sine)
    cotangent_of_projection = jnp.concatenate(
        [
            unrotated_key.reshape(sequence_length, KEY_VALUE_HEADS * HEAD_DIMENSION),
            cotangent_of_value.reshape(sequence_length, KEY_VALUE_HEADS * HEAD_DIMENSION),
        ],
        axis=1,
    ).astype(jnp.bfloat16)
    normed_gradient = lax.dot_general(
        cotangent_of_projection,
        lax.all_gather(weight_rows, "fsdp", axis=0, tiled=True),
        (((1,), (1,)), ((), ())),
        preferred_element_type=jnp.float32,
    )
    weight_term = lax.dot_general(
        normed_piece,
        cotangent_of_projection,
        (((0,), (0,)), ((), ())),
        preferred_element_type=jnp.float32,
    )
    gain_term = jnp.sum(normed_gradient * wide * inverse, axis=0)
    upstream = normed_gradient * gain_piece.astype(jnp.float32)
    input_gradient = (
        inverse
        * (upstream - wide * inverse * inverse * jnp.mean(upstream * wide, axis=1, keepdims=True))
    ).astype(jnp.bfloat16)
    weight_share, gain_share = (
        lax.psum_scatter(
            weight_term.astype(jnp.bfloat16), "fsdp", scatter_dimension=0, tiled=True
        ).astype(jnp.float32),
        lax.psum_scatter(
            gain_term.astype(jnp.bfloat16), "fsdp", scatter_dimension=0, tiled=True
        ).astype(jnp.float32),
    )
    return (query_gradient, input_gradient, weight_share[None], gain_share[None])


def outer_step(fragment_local, fragment_master, fragment_moment):
    replicas = lax.axis_size("rep")
    local_wide = fragment_local[0].astype(jnp.float32)
    total = lax.psum_scatter(
        local_wide.astype(jnp.bfloat16), "rep", scatter_dimension=1, tiled=True
    ).astype(jnp.float32)
    replica_mean = total / replicas
    pseudo = fragment_master - replica_mean
    moment_next = outer_momentum * fragment_moment + pseudo
    master_next = fragment_master - outer_rate * (pseudo + outer_momentum * moment_next)
    master_half = master_next.astype(jnp.bfloat16)
    master_whole = lax.all_gather(master_half, "rep", axis=1, tiled=True)
    fragment_next = (
        mixing * local_wide + (1.0 - mixing) * master_whole.astype(jnp.float32)
    ).astype(jnp.bfloat16)
    return (master_next, moment_next, fragment_next[None])


def on_device(
    activations,
    queries,
    attention_output_cotangent,
    document_ids,
    norm_gain,
    key_value_weight,
    fragment_local,
    fragment_master,
    fragment_moment,
):
    inner = inner_step(
        activations, queries, attention_output_cotangent, document_ids, norm_gain, key_value_weight
    )
    outer = outer_step(fragment_local, fragment_master, fragment_moment)
    return inner + outer


def solution(mesh):
    placed = (
        P(("rep", "fsdp"), None),
        P(("rep", "fsdp"), None),
        P(("rep", "fsdp"), None),
        P(("rep", "fsdp"), None),
        P("rep", "fsdp"),
        P("rep", "fsdp", None),
        P("rep", "fsdp", None),
        P("fsdp", "rep"),
        P("fsdp", "rep"),
    )
    return jax.shard_map(
        on_device,
        mesh=mesh,
        in_specs=placed,
        out_specs=(
            P(("rep", "fsdp"), None),
            P(("rep", "fsdp"), None),
            P("rep", "fsdp", None),
            P("rep", "fsdp"),
            P("fsdp", "rep"),
            P("fsdp", "rep"),
            P("rep", "fsdp", None),
        ),
        check_vma=False,
    )
```

profile of v0, /device:TPU:6, one launch (start us, length us, event | category | flops | bytes accessed | tf_op | source)
XLA Modules:
  0.0 351.7 jit_solution(8483838130947761575)
XLA Ops:
  8.0 0.0 copy-start.8
  8.0 0.0 all-gather.4.cloned.1.call-start
  8.1 0.7 all-gather.4.cloned.1.call-update
  8.8 0.0 reduce-scatter.7.cloned.1.call-start
  8.8 2.0 copy.99
  10.8 0.0 reduce-scatter.7.cloned.1.call-update
  10.9 0.0 reduce-scatter.5.cloned.1.call-start
  10.9 0.8 compare_reduce_fusion
  11.8 0.1 bitcast_select_fusion.4
  11.9 0.3 reduce-window.9
  12.2 0.1 slice.37
  12.3 0.1 slice_reduce_fusion
  12.4 0.1 fusion.47
  12.5 2.1 fusion.17
  14.6 36.4 %all-gather = bf16[1,4096]{1,0:T(2,128)(2,1)S(1)} all-gather(bf16[1,256]{1,0:T(2,128)(2,1)S(1)} %copy-done.9), channel_id=2, replica_groups=mesh['rep'=16,'fsdp'=16] {'fsdp'}, dimensions={1}, use_global_device_ids=true | all-gather | bytes 8704 | tf_op jit(solution)/shard_map/all_gather | solution.py:99
  51.0 0.1 fusion.46
  51.1 0.0 copy-start
  51.2 4.3 %copy.102 = bf16[256,4096]{0,1:T(8,128)(2,1)} copy(bf16[256,4096]{1,0:T(8,128)(2,1)} %param.10) | data formatting | bytes 4194304 | tf_op jit(solution)/shard_map/reshape | solution.py:54
  55.4 4.1 %copy.103 = bf16[256,4096]{0,1:T(8,128)(2,1)} copy(bf16[256,4096]{1,0:T(8,128)(2,1)} %param.11) | data formatting | bytes 4194304 | tf_op jit(solution)/shard_map/reshape | solution.py:55
  59.6 0.3 multiply_cosine_fusion
  59.9 54.9 %all-gather.4.cloned.1.call-done = bf16[1,4096,1024]{2,1,0:T(8,128)(2,1)} async-done(((bf16[1,256,1024]{2,1,0:T(8,128)(2,1)}), bf16[1,4096,1024]{2,1,0:T(8,128)(2,1)}) %all-gather.4.cloned.1.call-update) | async-done | bytes 8388624 | tf_op jit(solution)/shard_map/all_gather | solution.py:100
  114.8 5.8 %fusion.7 = f32[256,1024]{1,0:T(8,128)S(1)} fusion(bf16[1,4096,1024]{2,1,0:T(8,128)(2,1)} %all-gather.4.cloned.1.call-done, bf16[256,4096]{1,0:T(8,128)(2,1)S(1)} %copy-done, f32[4096]{0:T(1024)S(1)} %bitcast.123, f32[256]{0:T(256)S(1)} %add_rsqrt_fusion), kind=kOutput, calls=%fused_computation.10 | convolution fusion | flops 2151677952 | bytes 11551744 | tf_op jit(solution)/shard_map/dot_general | solution.py:102
  120.6 0.7 slice.56
  121.4 0.2 copy.101
  121.6 1.7 convert_element_type.74
  123.4 6.2 %fusion.44 = f32[4,256,256,8]{2,1,3,0:T(8,128)} fusion(bf16[256,4,8,128]{0,3,2,1:T(8,128)(2,1)} %bitcast.109, bf16[256,4,128,1]{2,1,0,3:T(4,128)(2,1)} %bitcast.120), kind=kOutput, calls=%fused_computation.57 | convolution fusion | flops 536870912 | bytes 10747904 | tf_op jit(solution)/shard_map/tkgd,skd->kgts/dot_general | solution.py:69
  129.5 0.8 fusion.43
  130.3 7.8 %fusion.60 = (f32[4,8,256]{2,1,0:T(8,128)S(1)}, f32[4,8,256,256]{2,3,1,0:T(8,128)}) fusion(pred[256,256]{0,1:T(8,128)(4,1)S(1)} %fusion.46, bf16[256,4,128,1]{0,2,3,1:T(8,128)(2,1)} %fusion.43, bf16[256,4,8,128]{0,3,2,1:T(8,128)(2,1)} %bitcast.114), kind=kOutput, calls=%fused_computation.89 | convolution fusion | flops 545259776 | bytes 10846208 | tf_op jit(solution)/shard_map/sub | solution.py:66
  138.1 6.2 %fusion.34 = bf16[4,256,128]{1,2,0:T(8,128)(2,1)} fusion(bf16[256,4,8,128]{0,3,2,1:T(8,128)(2,1)} %bitcast.110, f32[4,8,256,256]{2,3,1,0:T(8,128)} %get-tuple-element.47, f32[4,8,256]{2,1,0:T(8,128)S(1)} %get-tuple-element.46), kind=kOutput, calls=%fused_computation.42 | convolution fusion | flops 541196288 | bytes 10780672 | tf_op jit(solution)/shard_map/kgts,tkgd->skd/dot_general | solution.py:85
  144.3 13.8 %fusion.30 = f32[4,256,128]{1,2,0:T(8,128)S(1)} fusion(bf16[256,4,8,128]{0,3,2,1:T(8,128)(2,1)} %bitcast.115, f32[4,256,256,8]{2,1,3,0:T(8,128)} %fusion.44, f32[4,8,256,256]{2,3,1,0:T(8,128)} %get-tuple-element.47, f32[4,8,256]{2,1,0:T(8,128)S(1)} %get-tuple-element.46), kind=kOutput, calls=%fused_computation.40 | convolution fusion | flops 551559424 | bytes 19431424 | tf_op jit(solution)/shard_map/kgts,tkgd->skd/dot_general | solution.py:82
  158.2 0.1 fusion.42
  158.3 7.0 %convolution_convert_fusion = bf16[4096,1024]{1,0:T(8,128)(2,1)} fusion(bf16[256,4096]{1,0:T(8,128)(2,1)S(1)} %copy-done, f32[4096]{0:T(1024)S(1)} %bitcast.124, f32[256]{0:T(256)S(1)} %add_rsqrt_fusion, bf16[256,512]{0,1:T(8,128)(2,1)} %bitcast.121, bf16[256,512]{0,1:T(8,128)(2,1)S(1)} %bitcast.118), kind=kOutput, calls=%fused_computation.13 | convolution fusion | flops 2156920832 | bytes 11027456 | tf_op jit(solution)/shard_map/dot_general | solution.py:131
  165.3 0.0 copy-start.1
  165.3 0.0 reduce-scatter.5.cloned.1.call-update
  165.3 0.6 copy-done.10
  165.9 0.6 dynamic-slice
  167.2 0.0 reduce-scatter.7.cloned.1.call-done
  167.2 1.4 fusion.58
  168.7 107.4 %all_gather.12 = bf16[256,1024]{0,1:T(8,128)(2,1)} all-gather(bf16[256,64]{0,1:T(8,128)(2,1)S(1)} %get-tuple-element.37), channel_id=1, replica_groups=mesh['rep'=16,'fsdp'=16] {'rep'}, dimensions={1}, use_global_device_ids=true | all-gather | bytes 557056 | tf_op jit(solution)/shard_map/all_gather | solution.py:165
  276.0 1.2 copy.85
  277.3 1.0 fusion.39
  278.3 14.7 %fusion.29 = bf16[4,128,8,256]{3,1,2,0:T(8,128)(2,1)} fusion(bf16[256,4,128,1]{0,2,3,1:T(8,128)(2,1)S(1)} %copy-done.5, f32[4,256,256,8]{2,1,3,0:T(8,128)} %fusion.44, f32[4,8,256,256]{2,3,1,0:T(8,128)} %get-tuple-element.47, f32[4,8,256]{2,1,0:T(8,128)S(1)} %get-tuple-element.46), kind=kOutput, calls=%fused_computation.39 | convolution fusion | flops 552608000 | bytes 19169280 | tf_op jit(solution)/shard_map/kgts,skd->tkgd/dot_general | solution.py:76
  293.0 4.1 %copy.86 = bf16[256,4096]{1,0:T(8,128)(2,1)} copy(bf16[256,4096]{0,1:T(8,128)(2,1)} %bitcast.116) | data formatting | bytes 4194304
  297.1 8.4 %fusion.20 = (bf16[4096]{0:T(1024)(128)(2,1)S(1)}, f32[256]{0:T(256)S(1)}, f32[256,4096]{1,0:T(8,128)}) fusion(bf16[256,4096]{1,0:T(8,128)(2,1)S(1)} %copy-done, f32[256]{0:T(256)S(1)} %add_rsqrt_fusion, f32[4096]{0:T(1024)S(1)} %bitcast.125, bf16[1,4096,1024]{2,1,0:T(8,128)(2,1)} %all-gather.4.cloned.1.call-done, bf16[256,512]{0,1:T(8,128)(2,1)S(1)} %bitcast.122, ...), kind=kOutput, calls=%fused_computation.29 | convolution fusion | flops 2155867904 | bytes 15230976 | tf_op jit(solution)/shard_map/dot_general | solution.py:125
  305.5 31.1 %all-reduce = bf16[4096]{0:T(1024)(128)(2,1)S(1)} all-reduce(bf16[4096]{0:T(1024)(128)(2,1)S(1)} %get-tuple-element.35), channel_id=5, replica_groups=mesh['rep'=16,'fsdp'=16] {'fsdp'}, use_global_device_ids=true, to_apply=%region_9.10.clone | all-reduce | flops 4096 | bytes 16384
  336.7 0.6 dynamic-slice_convert_fusion
  337.3 4.8 %fusion.16 = bf16[256,4096]{1,0:T(8,128)(2,1)} fusion(bf16[256,4096]{1,0:T(8,128)(2,1)S(1)} %copy-done, f32[256,4096]{1,0:T(8,128)} %get-tuple-element.48, f32[256]{0:T(256)S(1)} %broadcast_multiply_fusion, f32[4096]{0:T(1024)S(1)} %bitcast.126, f32[256]{0:T(256)S(1)} %add_rsqrt_fusion), kind=kLoop, calls=%fused_computation.25 | loop fusion | flops 8388608 | bytes 8407040 | tf_op jit(solution)/shard_map/convert_element_type | solution.py:142
  342.1 2.1 bitcast_convert_fusion
  (29 shorter events, 0.3 us)
Async XLA Ops:
  8.0 43.0 %copy-start.8 = (s32[1,256]{1,0:T(1,128)S(1)}, s32[1,256]{1,0:T(1,128)}, u32[]{:S(2)}) copy-start(s32[1,256]{1,0:T(1,128)} %param.12) | copy-start | bytes 3076
  8.0 6.6 %copy-start.9 = (bf16[1,256]{1,0:T(2,128)(2,1)S(1)}, bf16[1,256]{1,0:T(2,128)(2,1)}, u32[]{:S(2)}) copy-start(bf16[1,256]{1,0:T(2,128)(2,1)} %param.13) | copy-start | bytes 1540
  8.0 106.8 %all-gather.4.cloned.1.call-start = ((), (), s32[]{:S(2)}) async-start(), calls=%async_computation.3 | async-start | bytes 8912896 | tf_op jit(solution)/shard_map/all_gather | solution.py:100
  8.8 158.4 %reduce-scatter.7.cloned.1.call-start = ((), (), s32[]{:S(2)}) async-start(), calls=%async_computation.4 | async-start | bytes 557056
  10.9 331.2 %reduce-scatter.5.cloned.1.call-start = ((), (), s32[]{:S(2)}) async-start(), calls=%async_computation.2 | async-start | bytes 8912896 | tf_op jit(solution)/shard_map/reduce_scatter | solution.py:144
  51.1 63.7 %copy-start = (bf16[256,4096]{1,0:T(8,128)(2,1)S(1)}, bf16[256,4096]{1,0:T(8,128)(2,1)}, u32[]{:S(2)}) copy-start(bf16[256,4096]{1,0:T(8,128)(2,1)} %param.9) | copy-start | bytes 6291460
  158.3 7.0 %copy-start.2 = (bf16[256,4,128]{0,2,1:T(8,128)(2,1)}, bf16[256,4,128]{0,2,1:T(8,128)(2,1)S(1)}, u32[]{:S(2)}) copy-start(bf16[256,4,128]{0,2,1:T(8,128)(2,1)S(1)} %fusion.42) | copy-start | bytes 786436
  165.3 0.7 copy-start.10
  165.3 1.9 copy-start.6
  165.3 2.0 copy-start.7
  165.3 112.0 %copy-start.1 = (bf16[1,256,1024]{2,1,0:T(8,128)(2,1)S(1)}, bf16[1,256,1024]{2,1,0:T(8,128)(2,1)}, u32[]{:S(2)}) copy-start(bf16[1,256,1024]{2,1,0:T(8,128)(2,1)} %param.15) | copy-start | bytes 1572868
  165.3 113.0 %copy-start.5 = (bf16[256,4,128,1]{0,2,3,1:T(8,128)(2,1)S(1)}, bf16[256,4,128,1]{0,2,3,1:T(8,128)(2,1)}, u32[]{:S(2)}) copy-start(bf16[256,4,128,1]{0,2,3,1:T(8,128)(2,1)} %fusion.43) | copy-start | bytes 786436
  293.0 4.1 %copy-start.3 = (bf16[256,4,128]{0,2,1:T(8,128)(2,1)S(1)}, bf16[256,4,128]{0,2,1:T(8,128)(2,1)}, u32[]{:S(2)}) copy-start(bf16[256,4,128]{0,2,1:T(8,128)(2,1)} %copy-done.2) | copy-start | bytes 786436
  293.0 4.1 %copy-start.4 = (bf16[4,256,128]{1,2,0:T(8,128)(2,1)S(1)}, bf16[4,256,128]{1,2,0:T(8,128)(2,1)}, u32[]{:S(2)}) copy-start(bf16[4,256,128]{1,2,0:T(8,128)(2,1)} %fusion.34) | copy-start | bytes 786436
Sparse Core Ops, SparseCore 0:
  10.6 104.1 all-gather.3
Sparse Core Ops, SparseCore 1:
  13.8 128.2 reduce-scatter.6
  165.4 99.4 reduce-scatter.4
where the time goes:
time: 354 us; the launch traced here: 352 us
  blocking collectives  175 us (49%)
  matrix products  69.7 us (20%)
  waiting for transfers between devices  55.7 us (16%)
  local copies, waits for them, and re-layouts  19.9 us (6%)
  between operations  16.4 us (5%)
  other arithmetic  14.9 us (4%)
    all_gather x1, blocking collectives, outer_step(): master_whole = lax.all_gather(master_half, 'rep', axis=1, tiled=True)  107 us
    all_gather x1, waiting for transfers between devices, inner_step(): weight_piece = lax.all_gather(weight_rows, 'fsdp', axis=0, tiled=True)  54.9 us
    all_gather x1, blocking collectives, inner_step(): gain_piece = lax.all_gather(gain_rows, 'fsdp', axis=0, tiled=True)  36.4 us
    unnamed x1, blocking collectives  31.1 us
    dot_general x1, matrix products, attention_terms(): jnp.einsum('kgts,skd->tkgd', score_cotangent, keys, preferred_element_typ...  14.7 us
    dot_general x1, matrix products, attention_terms(): jnp.einsum('kgts,tkgd->skd', score_cotangent, heads_of_query, preferred_e...  13.8 us
    dot_general x1, matrix products, inner_step(): lax.dot_general(cotangent_of_projection, lax.all_gather(weight_rows, 'fsd...  8.41 us
    sub x1, matrix products, attention_terms(): exponent = jnp.exp(scores - highest)  7.79 us
  transfers between devices with their start and end apart: 3, of which 1 were waited for; matrix products, arithmetic and copies ran while one was open for 29% of the time, Pallas kernels for 0%

commit v1 on v0

v1 whole, which is shorter than its diff:
```python
import math

import jax
import jax.numpy as jnp
from jax import lax
from jax.experimental import pallas as pl
from jax.experimental.pallas import tpu as pltpu
from jax.sharding import PartitionSpec as P

epsilon = 1e-05
rope_base = 500000.0
outer_rate = 0.7
outer_momentum = 0.9
mixing = 0.5
masked_score = -1e30

TOK = 256
WIDE = 4096
HALF = 2048
GROUPS = 4
PAIRS = 4
HD = 128
RING = 8
SCALE = HD ** (-0.5)
EXP2_SCALE = SCALE * math.log2(math.e)
PIECE = 512
PIECES = HALF // PIECE

f32 = jnp.float32
bf16 = jnp.bfloat16
NT = (((1,), (1,)), ((), ()))


def dot(a, b):
    return jnp.dot(a, b, preferred_element_type=f32)


def dot_nt(a, b):
    return lax.dot_general(a, b, NT, preferred_element_type=f32)


def kernel(
    x_ref, q_ref, do_ref, doc_ref, gain_ref, w_ref, fl_ref, fm_ref, fmo_ref,
    dq_out, dx_out, dw_out, dg_out, mn_out, mo_out, fn_out,
    X, XO, XT, Q, DO, WR, WB, PIN, POUT, PRAW, E, UOUT, UIN, DX, RB, SB, DW,
    INV, CO, COS, SIN, BLO, BHI, KB, VB, KT, DKA, DVA, GC, DG,
    F, FS, FSUM, XR, YS, YR, MW, FN, M0, M1, MB, MSB, R1, R2, MN, MO,
    ag_s, ag_r, rs_s, rs_r, x_s, x_r, p_s, p_r, e_s, e_r, u_s, u_r, o_s, o_r, l_s,
):
    f = lax.axis_index("fsdp")
    r = lax.axis_index("rep")
    z = lax.rem(f, RING)
    h = lax.div(f, RING)
    core = lax.rem(r, 2)
    yh = lax.rem(lax.div(r, 2), 2)
    xx = lax.div(r, 4)

    right = {"fsdp": h * RING + lax.rem(z + 1, RING)}
    left = {"fsdp": h * RING + lax.rem(z + RING - 1, RING)}
    partner = {"fsdp": (1 - h) * RING + z}
    sibling = {"rep": xx * 4 + yh * 2 + (1 - core)}
    across = {"rep": xx * 4 + (1 - yh) * 2 + core}
    xpeer = [{"rep": lax.rem(xx + j, 4) * 4 + yh * 2 + core} for j in (1, 2, 3)]

    def remote(src, dst, ssem, rsem, device):
        return pltpu.make_async_remote_copy(
            src_ref=src, dst_ref=dst, send_sem=ssem, recv_sem=rsem,
            device_id=device, device_id_type=pl.DeviceIdType.MESH,
        )

    def al(value, m):
        return pl.multiple_of(value, m)

    mine = pl.ds(al(h * HALF, HALF), HALF)
    other = pl.ds(al((1 - h) * HALF, HALF), HALF)
    ld_w = pltpu.make_async_copy(w_ref.at[0], WR, l_s.at[0])
    ld_x = pltpu.make_async_copy(x_ref.at[:, mine], X.at[0:TOK], l_s.at[1])
    ld_xo = pltpu.make_async_copy(x_ref.at[:, other], XO, l_s.at[2])
    ld_q = pltpu.make_async_copy(q_ref, Q, l_s.at[3])
    ld_do = pltpu.make_async_copy(do_ref, DO, l_s.at[4])
    ld_f = pltpu.make_async_copy(fl_ref.at[0], F, l_s.at[5])
    ld_m0 = pltpu.make_async_copy(fm_ref, M0, l_s.at[6])
    ld_m1 = pltpu.make_async_copy(fmo_ref, M1, l_s.at[7])
    for c in (ld_w, ld_x, ld_xo, ld_f, ld_m0, ld_m1, ld_q, ld_do):
        c.start()

    barrier = pltpu.get_barrier_semaphore()
    for d in (left, right, partner, sibling, across, *xpeer):
        pl.semaphore_signal(barrier, inc=1, device_id=d, device_id_type=pl.DeviceIdType.MESH)
    pl.semaphore_wait(barrier, 8)

    def x_copy(j):
        return remote(
            x_ref.at[:, pl.ds(al((1 - h) * HALF + j * PIECE, PIECE), PIECE)],
            X.at[TOK : 2 * TOK, j * PIECE : (j + 1) * PIECE],
            x_s.at[j], x_r.at[j], partner,
        )

    for j in range(PIECES):
        x_copy(j).start()

    def ring_at(dist):
        return lax.rem(z + dist + 2 * RING, RING)

    def ag_sem(d, g, s):
        return d * 16 + g * 4 + (s - 1)

    def ag_copy(d, g, s, shard):
        start, size = (shard * TOK, TOK) if s < 4 else (shard * TOK + d * 128, 128)
        block = WB.at[g, pl.ds(al(start, 128), size)]
        i = ag_sem(d, g, s)
        return remote(block, block, ag_s.at[i], ag_r.at[i], (right, left)[d])

    def ag_send(d, g, s):
        return ag_copy(d, g, s, ring_at((1 - s) if d == 0 else (s - 1)))

    def ag_recv(d, g, s):
        return ag_copy(d, g, s, ring_at(-s if d == 0 else s))

    def ag_step(g, s):
        for d in (0, 1):
            ag_recv(d, g, s).wait_recv()
            if s < 4:
                ag_send(d, g, s + 1).start()

    eye = lax.broadcasted_iota(jnp.int32, (TOK, TOK), 0) == lax.broadcasted_iota(jnp.int32, (TOK, TOK), 1)

    def column(row):
        square = jnp.where(eye, jnp.broadcast_to(row, (TOK, TOK)), 0.0).astype(bf16)
        return dot(square, jnp.ones((TOK, HD), bf16))

    gain_row = gain_ref[...].astype(f32)
    gain = column(gain_row)
    GC[...] = gain
    ld_w.wait()
    own_rows = pl.ds(al(z * TOK, TOK), TOK)

    def scale_w(g):
        WB[g, own_rows, 0:HD] = (WR[:, g * HD : (g + 1) * HD].astype(f32) * gain).astype(bf16)
        WB[g, own_rows, HD : 2 * HD] = (
            WR[:, 512 + g * HD : 512 + (g + 1) * HD].astype(f32) * gain
        ).astype(bf16)

    for g in (0, 1):
        scale_w(g)
        for d in (0, 1):
            ag_send(d, g, 1).start()
    for g in (2, 3):
        scale_w(g)

    rows_k = pl.ds(al(core * 128, 128), 128)
    rows_o = pl.ds(al((1 - core) * 128, 128), 128)
    lane = lax.broadcasted_iota(jnp.int32, (128, 128), 1)
    low = lane < 64
    block_c = pl.ds(al((2 * xx + yh) * 128, 128), 128)
    block_x = pl.ds(al(xx * 256, 256), 256)

    def swap(v):
        return pltpu.roll(v, 64, 1)

    o_frag = remote(F.at[rows_o], FS, o_s.at[0], o_r.at[0], sibling)
    o_state = remote(MB.at[rows_o], MSB, o_s.at[1], o_r.at[1], sibling)

    def o_x(j):
        to = lax.rem(xx + j + 1, 4)
        return remote(
            FSUM.at[:, pl.ds(al(to * 256, 256), 256)], XR.at[j], o_s.at[2 + j], o_r.at[2 + j], xpeer[j]
        )

    o_y = remote(YS, YR, o_s.at[5], o_r.at[5], across)
    o_pack = remote(R1, R2, o_s.at[6], o_r.at[6], sibling)

    def mw(rows, cols, i, device):
        return remote(MW.at[rows, cols], MW.at[rows, cols], o_s.at[i], o_r.at[i], device)

    o_back_y = mw(rows_k, block_c, 7, across)
    block_c_across = pl.ds(al((2 * xx + 1 - yh) * 128, 128), 128)
    o_back_y_in = mw(rows_k, block_c_across, 7, across)

    def o_back_x(j):
        return mw(rows_k, block_x, 8 + j, xpeer[j])

    def o_back_x_in(j):
        frm = lax.rem(xx + 4 - (j + 1), 4)
        return mw(rows_k, pl.ds(al(frm * 256, 256), 256), 8 + j, xpeer[j])

    o_back_s = mw(rows_k, slice(None), 11, sibling)
    o_back_s_in = mw(rows_o, slice(None), 11, sibling)

    def outer_1():
        ld_f.wait()
        ld_m0.wait()
        ld_m1.wait()
        MB[...] = jnp.concatenate([M0[...], M1[...]], axis=1)
        o_frag.start()
        o_state.start()

    def outer_2():
        o_frag.wait_recv()
        FSUM[...] = (F[rows_k, :].astype(f32) + FS[...].astype(f32)).astype(bf16)
        for j in range(3):
            o_x(j).start()

    def outer_3():
        for j in range(3):
            o_x(j).wait_recv()
        total = FSUM[:, block_x].astype(f32)
        for j in range(3):
            total = total + XR[j].astype(f32)
        first, second = total[:, 0:128], total[:, 128:256]
        YS[...] = jnp.where(yh == 0, second, first).astype(bf16)
        R1[...] = jnp.where(yh == 0, first, second)
        o_y.start()

    def outer_4():
        o_y.wait_recv()
        o_state.wait_recv()
        mean = (R1[...] + YR[...].astype(f32)) * (1.0 / 16.0)
        own, sib = MB[rows_k, :], MSB[...]
        a = jnp.where(core == 0, own, sib)
        b = jnp.where(core == 0, sib, own)
        master = jnp.where(low, a, swap(b))
        moment = jnp.where(low, swap(a), b)
        pseudo = master - mean
        moment_next = outer_momentum * moment + pseudo
        master_next = master - outer_rate * (pseudo + outer_momentum * moment_next)
        MW[rows_k, block_c] = master_next.astype(bf16)
        o_back_y.start()
        pack_0 = jnp.where(low, master_next, swap(moment_next))
        pack_1 = jnp.where(low, swap(master_next), moment_next)
        R1[...] = jnp.where(core == 0, pack_1, pack_0)
        o_pack.start()
        keep = jnp.where(core == 0, pack_0, pack_1)
        MN[rows_k, :] = keep[:, 0:64]
        MO[rows_k, :] = keep[:, 64:128]

    def outer_5():
        o_back_y_in.wait_recv()
        for j in range(3):
            o_back_x(j).start()
        o_pack.wait_recv()
        MN[rows_o, :] = R2[:, 0:64]
        MO[rows_o, :] = R2[:, 64:128]
        st_mn.start()
        st_mo.start()

    def outer_6():
        for j in range(3):
            o_back_x_in(j).wait_recv()
        o_back_s.start()

    def outer_7():
        o_back_s_in.wait_recv()
        FN[...] = (mixing * F[...].astype(f32) + (1.0 - mixing) * MW[...].astype(f32)).astype(bf16)
        st_fn.start()

    st_mn = pltpu.make_async_copy(MN, mn_out, l_s.at[8])
    st_mo = pltpu.make_async_copy(MO, mo_out, l_s.at[9])
    st_fn = pltpu.make_async_copy(FN, fn_out.at[0], l_s.at[10])

    def tables():
        doc_row = doc_ref[...].astype(f32)
        doc = column(doc_row)
        doc2 = jnp.concatenate([doc, doc], axis=1)
        row = jnp.broadcast_to(doc_row, (TOK, TOK))
        before = jnp.sum(jnp.where(row < doc2, 1.0, 0.0), axis=1, keepdims=True)
        token = lax.broadcasted_iota(jnp.int32, (TOK, HD), 0).astype(f32)
        position = token - before
        i = lax.broadcasted_iota(jnp.int32, (TOK, HD), 1)
        half = jnp.where(i < 64, i, i - 64).astype(f32)
        angle = position * jnp.exp(half * (-2.0 / HD * math.log(rope_base)))
        COS[...] = jnp.cos(angle)
        SIN[...] = jnp.where(i < 64, -1.0, 1.0) * jnp.sin(angle)
        u = lax.broadcasted_iota(jnp.int32, (TOK, TOK), 0)
        t = lax.broadcasted_iota(jnp.int32, (TOK, TOK), 1)
        bias = jnp.where((u <= t) & (row == doc2), 0.0, masked_score)
        BLO[...] = jnp.concatenate([bias[0:128, 0:128], bias[0:128, 0:128]], axis=1)
        BHI[...] = jnp.concatenate([bias[:, 128:256], bias[:, 128:256]], axis=1)

    def inverse():
        ld_x.wait()
        ld_xo.wait()
        a = X[0:TOK, :].astype(f32)
        total = jnp.sum(a * a, axis=1, keepdims=True)
        b = XO[...].astype(f32)
        total = total + jnp.sum(b * b, axis=1, keepdims=True)
        INV[...] = jnp.broadcast_to(lax.rsqrt(total * (1.0 / WIDE) + epsilon), (TOK, HD))
        CO[...] = jnp.zeros_like(CO)

    def transpose_x(who, j):
        XT[j * PIECE : (j + 1) * PIECE, who * TOK : (who + 1) * TOK] = X[
            who * TOK : (who + 1) * TOK, j * PIECE : (j + 1) * PIECE
        ].T

    def p_copy(g):
        return remote(POUT.at[g], PIN.at[g], p_s.at[g], p_r.at[g], partner)

    def project(g):
        POUT[g] = dot(X[TOK : 2 * TOK, :], WB[g]).astype(bf16)
        p_copy(g).start()
        PRAW[g] = dot(X[0:TOK, :], WB[g])

    def e_copy(g):
        return remote(E.at[g, 0:TOK], E.at[g, TOK : 2 * TOK], e_s.at[g], e_r.at[g], partner)

    def group_start(g):
        p_copy(g).wait_recv()
        raw = PRAW[g] + PIN[g].astype(f32)
        PRAW[g] = raw
        inv = INV[...]
        k = raw[:, 0:HD] * inv
        k = k * COS[...] + pltpu.roll(k, 64, 1) * SIN[...]
        kb = k.astype(bf16)
        KB[...] = kb
        KT[...] = kb.T
        VB[...] = (raw[:, HD : 2 * HD] * inv).astype(bf16)
        DKA[...] = jnp.zeros_like(DKA)
        DVA[...] = jnp.zeros_like(DVA)

    def group_end(g):
        dk = DKA[...] * SCALE
        inv = INV[...]
        dk = dk * COS[...] - pltpu.roll(dk, 64, 1) * SIN[...]
        ek = (dk * inv).astype(bf16)
        ev = (DVA[...] * inv).astype(bf16)
        E[g, 0:TOK, 0:HD] = ek
        E[g, 0:TOK, HD : 2 * HD] = ev
        e_copy(g).start()
        raw = PRAW[g]
        part = ek.astype(f32) * raw[:, 0:HD] + ev.astype(f32) * raw[:, HD : 2 * HD]
        CO[...] += jnp.broadcast_to(jnp.sum(part, axis=1, keepdims=True), (TOK, HD))

    def attend(kb, vb, kt, qc, dc, bias):
        s = dot_nt(kb, qc) + bias
        w = dot_nt(vb, dc)
        top = jnp.max(s, axis=0, keepdims=True)
        e = jnp.exp2((s - top) * EXP2_SCALE)
        p = e * (1.0 / jnp.sum(e, axis=0, keepdims=True))
        pw = p * w
        delta = jnp.sum(pw, axis=0, keepdims=True)
        ds = (pw - p * delta).astype(bf16)
        dq = (dot(kt, ds) * SCALE).T.astype(bf16)
        return dq, dot(ds, qc), dot(p.astype(bf16), dc)

    def head_pair(column_start):
        ca = pl.ds(al(column_start, 256), HD)
        cb = pl.ds(al(column_start + HD, HD), HD)
        low_rows, high_rows = slice(0, 128), slice(128, 256)

        def both(ref, rows):
            return jnp.concatenate([ref[rows, ca], ref[rows, cb]], axis=0)

        dq, dk, dv = attend(
            KB[...], VB[...], KT[...], both(Q, high_rows), both(DO, high_rows), BHI[...]
        )
        Q[high_rows, ca] = dq[0:128]
        Q[high_rows, cb] = dq[128:256]
        DKA[...] += dk
        DVA[...] += dv
        dq, dk, dv = attend(
            KB[low_rows, :], VB[low_rows, :], KT[:, low_rows],
            both(Q, low_rows), both(DO, low_rows), BLO[...],
        )
        Q[low_rows, ca] = dq[0:128]
        Q[low_rows, cb] = dq[128:256]
        DKA[low_rows, :] += dk
        DVA[low_rows, :] += dv

    def dq_store(g):
        cols = pl.ds(al(g * 1024, 1024), 1024)
        return pltpu.make_async_copy(Q.at[:, cols], dq_out.at[:, cols], l_s.at[11 + g])

    def rs_copy(d, g, s):
        i = ag_sem(d, g, s)
        if s == 1:
            rows = slice(d * 128, d * 128 + 128)
            src, dst = SB.at[i, rows], RB.at[i, rows]
        else:
            src, dst = SB.at[i], RB.at[i]
        return remote(src, dst, rs_s.at[i], rs_r.at[i], (right, left)[d])

    def term(owner, g):
        return dot(XT[pl.ds(al(owner * TOK, TOK), TOK), :], E[g])

    def rs_step(g, s):
        for d in (0, 1):
            owner = ring_at(5 - s if d == 0 else s - 5)
            i = ag_sem(d, g, s)
            if s == 1:
                start = al(owner * TOK + d * 128, 128)
                SB[i, d * 128 : d * 128 + 128] = dot(XT[pl.ds(start, 128), :], E[g]).astype(bf16)
            else:
                total = term(owner, g)
                rs_copy(d, g, s - 1).wait_recv()
                if s == 2:
                    came = slice(d * 128, d * 128 + 128)
                    rest = slice((1 - d) * 128, (1 - d) * 128 + 128)
                    SB[i, came] = (total[came] + RB[i - 1, came].astype(f32)).astype(bf16)
                    SB[i, rest] = total[rest].astype(bf16)
                else:
                    SB[i] = (total + RB[i - 1].astype(f32)).astype(bf16)
            rs_copy(d, g, s).start()

    def rs_end(g):
        total = term(z, g)
        for d in (0, 1):
            rs_copy(d, g, 4).wait_recv()
            total = total + RB[ag_sem(d, g, 4)].astype(f32)
        ck, cv = g * HD, 512 + g * HD
        wide_gain = GC[...]
        tk, tv = total[:, 0:HD], total[:, HD : 2 * HD]
        DW[:, ck : ck + HD] = tk * wide_gain
        DW[:, cv : cv + HD] = tv * wide_gain
        part = tk * WR[:, ck : ck + HD].astype(f32) + tv * WR[:, cv : cv + HD].astype(f32)
        return jnp.sum(part, axis=1, keepdims=True)

    def u_copy(j):
        return remote(UOUT.at[j], UIN.at[j], u_s.at[j], u_r.at[j], partner)

    def upstream(first, j):
        rows = slice(j * PIECE, (j + 1) * PIECE)
        total = dot_nt(E[0, first : first + TOK], WB[0, rows])
        for g in range(1, GROUPS):
            total = total + dot_nt(E[g, first : first + TOK], WB[g, rows])
        return total

    def dx_store(part, j):
        start = al((h if part == 0 else 1 - h) * HALF + j * PIECE, PIECE)
        return pltpu.make_async_copy(
            DX.at[part * PIECES + j], dx_out.at[:, pl.ds(start, PIECE)], l_s.at[15 + part * PIECES + j]
        )

    def send_upstream(j):
        UOUT[j] = upstream(TOK, j).astype(bf16)
        u_copy(j).start()

    def finish(part, j, u):
        cols = slice(j * PIECE, (j + 1) * PIECE)
        x = X[0:TOK, cols] if part == 0 else XO[:, cols]
        c = CO[...]
        c = jnp.concatenate([c] * (PIECE // HD), axis=1)
        DX[part * PIECES + j] = (u - x.astype(f32) * c).astype(bf16)
        dx_store(part, j).start()

    outer_1()
    tables()
    ag_step(0, 1)
    outer_2()
    ag_step(1, 1)
    inverse()
    ag_step(0, 2)
    transpose_x(0, 0)
    transpose_x(0, 1)
    ag_step(1, 2)
    transpose_x(0, 2)
    transpose_x(0, 3)
    outer_3()
    ag_step(0, 3)
    x_copy(0).wait_recv()
    transpose_x(1, 0)
    ag_step(1, 3)
    for g in (2, 3):
        for d in (0, 1):
            ag_send(d, g, 1).start()
    outer_4()
    x_copy(1).wait_recv()
    transpose_x(1, 1)
    ag_step(0, 4)
    ag_step(1, 4)
    outer_5()
    x_copy(2).wait_recv()
    transpose_x(1, 2)
    x_copy(3).wait_recv()
    project(0)
    project(1)
    transpose_x(1, 3)
    ld_q.wait()
    ld_do.wait()

    def attention(base, hook):
        def step(n, _):
            g = base + lax.div(n, PAIRS)
            part = lax.rem(n, PAIRS)

            @pl.when(part == 0)
            def _():
                group_start(g)

            head_pair((base * PAIRS + n) * 2 * HD)

            @pl.when(part == PAIRS - 1)
            def _():
                group_end(g)
                dq_store(g).start()

            hook(n)
            return 0

        lax.fori_loop(0, 2 * PAIRS, step, 0)

    def ag_hook(n):
        g, hop = 2 + lax.rem(n, 2), lax.div(n, 2)
        for s in (1, 2, 3, 4):

            @pl.when(hop == s - 1)
            def _(s=s):
                ag_step(g, s)

    def rs_hook(n):
        g, hop = lax.rem(n, 2), lax.div(n, 2)
        for s in (1, 2, 3, 4):

            @pl.when(hop == s - 1)
            def _(s=s):
                rs_step(g, s)

    attention(0, ag_hook)
    outer_6()
    project(2)
    project(3)
    for g in (0, 1):
        e_copy(g).wait_recv()
    attention(2, rs_hook)
    outer_7()
    e_copy(2).wait_recv()
    rs_step(2, 1)
    e_copy(3).wait_recv()
    rs_step(3, 1)
    CO[...] = CO[...] * INV[...] * INV[...] * (1.0 / WIDE)
    for j in range(PIECES):
        send_upstream(j)
    rs_step(2, 2)
    rs_step(3, 2)
    gain_total = rs_end(0)
    finish(0, 0, upstream(0, 0))
    rs_step(2, 3)
    rs_step(3, 3)
    gain_total = gain_total + rs_end(1)
    finish(0, 1, upstream(0, 1))
    rs_step(2, 4)
    rs_step(3, 4)
    finish(0, 2, upstream(0, 2))
    finish(0, 3, upstream(0, 3))
    for j in range(PIECES - 1):
        u_copy(j).wait_recv()
        finish(1, j, UIN[j].astype(f32))
    gain_total = gain_total + rs_end(2)
    gain_total = gain_total + rs_end(3)
    st_dw = pltpu.make_async_copy(DW, dw_out.at[0], l_s.at[23])
    st_dw.start()
    spread = jnp.where(eye, jnp.broadcast_to(gain_total, (TOK, TOK)), 0.0)
    DG[...] = jnp.sum(spread, axis=0, keepdims=True)
    st_dg = pltpu.make_async_copy(DG, dg_out, l_s.at[24])
    st_dg.start()
    u_copy(PIECES - 1).wait_recv()
    finish(1, PIECES - 1, UIN[PIECES - 1].astype(f32))

    for j in range(PIECES):
        x_copy(j).wait_send()
        u_copy(j).wait_send()

    def drain(g, _):
        p_copy(g).wait_send()
        e_copy(g).wait_send()
        for s in (1, 2, 3, 4):
            for d in (0, 1):
                ag_send(d, g, s).wait_send()
                rs_copy(d, g, s).wait_send()
        dq_store(g).wait()
        return 0

    lax.fori_loop(0, GROUPS, drain, 0)
    for c in (o_frag, o_state, o_y, o_pack, o_back_y, o_back_s):
        c.wait_send()
    for j in range(3):
        o_x(j).wait_send()
        o_back_x(j).wait_send()
    for part in (0, 1):
        for j in range(PIECES):
            dx_store(part, j).wait()
    for c in (st_mn, st_mo, st_fn, st_dw, st_dg):
        c.wait()


def on_device(x, q, do, doc, gain, w, fl, fm, fmo):
    sds = jax.ShapeDtypeStruct
    hbm = pl.BlockSpec(memory_space=pl.ANY)
    vmem = pl.BlockSpec(memory_space=pltpu.VMEM)

    def v(shape, t):
        return pltpu.VMEM(shape, t)

    dma = pltpu.SemaphoreType.DMA
    scratch = [
        v((2 * TOK, HALF), bf16),
        v((TOK, HALF), bf16),
        v((HALF, 2 * TOK), bf16),
        v((TOK, WIDE), bf16),
        v((TOK, WIDE), bf16),
        v((TOK, 1024), bf16),
        v((GROUPS, HALF, 256), bf16),
        v((GROUPS, TOK, 256), bf16),
        v((GROUPS, TOK, 256), bf16),
        v((GROUPS, TOK, 256), f32),
        v((GROUPS, 2 * TOK, 256), bf16),
        v((PIECES, TOK, PIECE), bf16),
        v((PIECES, TOK, PIECE), bf16),
        v((2 * PIECES, TOK, PIECE), bf16),
        v((32, TOK, 256), bf16),
        v((32, TOK, 256), bf16),
        v((TOK, 1024), f32),
        v((TOK, HD), f32),
        v((TOK, HD), f32),
        v((TOK, HD), f32),
        v((TOK, HD), f32),
        v((128, 256), f32),
        v((256, 256), f32),
        v((TOK, HD), bf16),
        v((TOK, HD), bf16),
        v((HD, TOK), bf16),
        v((TOK, HD), f32),
        v((TOK, HD), f32),
        v((TOK, HD), f32),
        v((1, TOK), f32),
        v((256, 1024), bf16),
        v((128, 1024), bf16),
        v((128, 1024), bf16),
        v((3, 128, 256), bf16),
        v((128, 128), bf16),
        v((128, 128), bf16),
        v((256, 1024), bf16),
        v((256, 1024), bf16),
        v((256, 64), f32),
        v((256, 64), f32),
        v((256, 128), f32),
        v((128, 128), f32),
        v((128, 128), f32),
        v((128, 128), f32),
        v((256, 64), f32),
        v((256, 64), f32),
        dma((32,)), dma((32,)), dma((32,)), dma((32,)),
        dma((4,)), dma((4,)), dma((4,)), dma((4,)),
        dma((4,)), dma((4,)), dma((4,)), dma((4,)),
        dma((12,)), dma((12,)), dma((25,)),
    ]
    return pl.pallas_call(
        kernel,
        out_shape=(
            sds((TOK, WIDE), bf16),
            sds((TOK, WIDE), bf16),
            sds((1, 256, 1024), f32),
            sds((1, 256), f32),
            sds((256, 64), f32),
            sds((256, 64), f32),
            sds((1, 256, 1024), bf16),
        ),
        in_specs=[hbm, hbm, hbm, vmem, vmem, hbm, hbm, hbm, hbm],
        out_specs=(hbm,) * 7,
        scratch_shapes=scratch,
        compiler_params=pltpu.CompilerParams(
            collective_id=0, has_side_effects=True, vmem_limit_bytes=48 * 2**20
        ),
        name="step",
    )(x, q, do, doc, gain, w, fl, fm, fmo)


def solution(mesh):
    placed = (
        P(("rep", "fsdp"), None),
        P(("rep", "fsdp"), None),
        P(("rep", "fsdp"), None),
        P(("rep", "fsdp"), None),
        P("rep", "fsdp"),
        P("rep", "fsdp", None),
        P("rep", "fsdp", None),
        P("fsdp", "rep"),
        P("fsdp", "rep"),
    )
    return jax.shard_map(
        on_device,
        mesh=mesh,
        in_specs=placed,
        out_specs=(
            P(("rep", "fsdp"), None),
            P(("rep", "fsdp"), None),
            P("rep", "fsdp", None),
            P("rep", "fsdp"),
            P("fsdp", "rep"),
            P("fsdp", "rep"),
            P("rep", "fsdp", None),
        ),
        check_vma=False,
    )
```

time: 354 us -> 129 us (0.36)
  blocking collectives: 175 us -> 0 us
  Pallas kernels: 0 us -> 113 us
  matrix products: 69.7 us -> 0 us
  waiting for transfers between devices: 55.7 us -> 0 us
  between operations: 16.4 us -> 0.68 us
  other arithmetic: 14.9 us -> 0 us
  local copies, waits for them, and re-layouts: 19.9 us -> 15.1 us
    all_gather x2 -> x0, blocking collectives: 144 us -> none  [the longest x1 107 us: outer_step(): master_whole = lax.all_gather(master_half, 'rep', axis=1, tiled=True)]
    pallas_call x0 -> x1, Pallas kernels: none -> 113 us  [on_device(): pl.pallas_call(kernel, out_shape=(sds((TOK, WIDE), bf16), sds((TOK, WIDE)...]
    dot_general x7 -> x0, matrix products: 62 us -> none  [the longest x1 14.7 us: attention_terms(): jnp.einsum('kgts,skd->tkgd', score_cotangent, keys, preferred_element_typ...]
    all_gather x1 -> x0, waiting for transfers between devices: 54.9 us -> none  [inner_step(): weight_piece = lax.all_gather(weight_rows, 'fsdp', axis=0, tiled=True)]
    unnamed x1 -> x0, blocking collectives: 31.1 us -> none
    reshape x3 -> x0, local copies, waits for them, and re-layouts: 8.59 us -> none  [the longest x1 4.28 us: attention_terms(): queries.reshape(sequence_length, KEY_VALUE_HEADS, query_group, HEAD_DIMEN...]
    sub x1 -> x0, matrix products: 7.79 us -> none  [attention_terms(): exponent = jnp.exp(scores - highest)]
    convert_element_type x5 -> x0, other arithmetic: 7.1 us -> none  [the longest x1 4.78 us: inner_step(): input_gradient = (inverse * (upstream - wide * inverse * inverse * jnp.me...]
  transfers between devices with their start and end apart: 3 -> 0, of which waited for: 1 -> 0; matrix products, arithmetic and copies ran while one was open for 29% -> 0% of each run, Pallas kernels for 0% -> 0%
where the time goes in v1:
time: 129 us
  Pallas kernels  113 us (88%)
  local copies, waits for them, and re-layouts  15.1 us (12%)
    pallas_call x1, Pallas kernels, on_device(): pl.pallas_call(kernel, out_shape=(sds((TOK, WIDE), bf16), sds((TOK, WIDE)...  113 us
    unnamed x23, local copies, waits for them, and re-layouts  12.7 us

profile of v1, /device:TPU:6, one launch (start us, length us, event | category | flops | bytes accessed | tf_op | source)
XLA Modules:
  0.0 128.6 jit_solution(3860700191561880503)
XLA Ops:
  0.6 0.9 copy.16.fm_ref
  1.6 0.9 copy.17.fmo_ref
  2.5 0.0 copy-start
  2.5 1.0 copy-done
  3.6 0.0 copy-start.1
  3.6 1.0 copy-done.1
  4.6 0.0 copy-start.5
  4.6 0.7 copy-done.5
  5.3 0.0 copy-start.6
  5.3 0.7 copy-done.6
  6.0 112.9 %step.1 = (bf16[256,4096]{1,0:T(8,128)(2,1)S(1)}, bf16[256,4096]{1,0:T(8,128)(2,1)}, f32[1,256,1024]{2,1,0:T(8,128)S(1)}, f32[1,256]{1,0:T(1,128)S(1)}, f32[256,...) custom-call(bf16[256,4096]{1,0:T(8,128)(2,1)} %x_ref.1, bf16[256,4096]{1,0:T(8,128)(2,1)} %q_ref.1, ...), custom_call_target="tpu_custom_call" | custom-call | tf_op jit(solution)/shard_map/step/pallas_call | solution.py:646
  118.8 0.0 copy-start.2
  118.8 0.8 copy-done.2
  119.6 0.0 copy-start.4
  119.6 0.7 copy-done.4
  120.3 1.6 %copy.18 = f32[256,64]{0,1:T(8,128)} copy(f32[256,64]{1,0:T(8,128)} %copy-done.4) | data formatting | bytes 131072 | tf_op jit(solution)/shard_map/step/pallas_call | solution.py:646
  121.9 0.7 copy.19
  122.6 0.0 copy-start.7
  122.6 1.3 %copy.25 = bf16[256,4096]{1,0:T(8,128)(2,1)} copy(bf16[256,4096]{1,0:T(8,128)(2,1)S(1)} %get-tuple-element.21) | data formatting | bytes 4194304
  123.9 1.0 copy-done.7
  125.0 1.3 %copy.26 = bf16[256,4096]{1,0:T(8,128)(2,1)} copy(bf16[256,4096]{1,0:T(8,128)(2,1)S(1)} %copy-done.7) | data formatting | bytes 4194304
  126.3 0.0 copy-start.3
  126.3 1.0 copy.27
  127.3 0.6 copy.28
  127.8 0.0 copy-done.3
  127.8 0.8 copy.29
Async XLA Ops:
  2.5 1.0 copy-start
  3.6 1.0 copy-start.1
  4.6 0.7 copy-start.5
  5.3 0.7 copy-start.6
  118.8 0.8 copy-start.2
  119.6 0.7 copy-start.4
  122.6 2.3 %copy-start.7 = (bf16[256,4096]{1,0:T(8,128)(2,1)S(1)}, bf16[256,4096]{1,0:T(8,128)(2,1)}, u32[]{:S(2)}) copy-start(bf16[256,4096]{1,0:T(8,128)(2,1)} %get-tuple-element.22) | copy-start | bytes 6291460
  126.3 1.5 %copy-start.3 = (bf16[1,256,1024]{2,1,0:T(8,128)(2,1)S(1)}, bf16[1,256,1024]{2,1,0:T(8,128)(2,1)}, u32[]{:S(2)}) copy-start(bf16[1,256,1024]{2,1,0:T(8,128)(2,1)} %copy-done.2) | copy-start | bytes 1572868

commit v2 on v1

--- a/solution.py
+++ b/solution.py
@@ -28,7 +28,70 @@
 
 f32 = jnp.float32
 bf16 = jnp.bfloat16
+VMEM_LIMIT = 40 * 2**20
 NT = (((1,), (1,)), ((), ()))
+
+
+BEFORE = (
+    ("inv",), ("tab",), ("tr", 0, 0), ("tr", 0, 1), ("tr", 0, 2), ("tr", 0, 3), ("o", 1), ("o", 2),
+    ("ag", 0, 0, 1), ("ag", 1, 0, 1), ("tr", 1, 0), ("ag", 0, 1, 1), ("ag", 1, 1, 1), ("ag", 0, 0, 2),
+    ("ag", 1, 0, 2), ("own", 2), ("o", 3), ("tr", 1, 1), ("ag", 0, 1, 2), ("ag", 1, 1, 2),
+    ("ag", 0, 0, 3), ("ag", 1, 0, 3), ("tr", 1, 2), ("ag", 0, 2, 1), ("ag", 1, 2, 1), ("own", 3),
+    ("ag", 0, 1, 3), ("ag", 1, 1, 3), ("ag", 0, 0, 4), ("ag", 1, 0, 4), ("po", 0), ("pp", 0),
+    ("tr", 1, 3), ("o", 4), ("ag", 0, 2, 2), ("ag", 1, 2, 2), ("ag", 0, 3, 1), ("ag", 1, 3, 1),
+    ("gs", 0),
+)
+DURING = (
+    (),
+    (
+        ("ag", 0, 1, 4), ("ag", 1, 1, 4), ("pp", 1), ("po", 1),
+    ),
+    (),
+    (
+        ("ag", 0, 2, 3), ("ag", 1, 2, 3),
+    ),
+    (
+        ("ge", 0), ("o", 5), ("gs", 1),
+    ),
+    (
+        ("ag", 0, 3, 2), ("ag", 1, 3, 2),
+    ),
+    (
+        ("ag", 0, 2, 4), ("ag", 1, 2, 4), ("pp", 2), ("po", 2),
+    ),
+    (
+        ("ew", 0), ("rs", 0, 0, 1), ("rs", 1, 0, 1),
+    ),
+    (
+        ("ge", 1), ("ag", 0, 3, 3), ("ag", 1, 3, 3), ("o", 6), ("gs", 2), ("rs", 0, 0, 2), ("rs", 1, 0, 2),
+    ),
+    (
+        ("ag", 0, 3, 4), ("ag", 1, 3, 4), ("pp", 3), ("po", 3),
+    ),
+    (
+        ("ew", 1), ("rs", 0, 1, 1), ("rs", 1, 1, 1),
+    ),
+    (
+        ("rs", 0, 0, 3), ("rs", 1, 0, 3),
+    ),
+    (
+        ("ge", 2), ("gs", 3), ("rs", 0, 1, 2), ("rs", 1, 1, 2),
+    ),
+    (),
+    (),
+    (
+        ("rs", 0, 0, 4), ("rs", 1, 0, 4),
+    ),
+)
+AFTER = (
+    ("ew", 2), ("ge", 3), ("rs", 0, 1, 3), ("rs", 1, 1, 3), ("rs", 0, 2, 1), ("rs", 1, 2, 1),
+    ("uo", 0), ("uo", 1), ("uo", 2), ("uo", 3), ("o", 7), ("re", 0), ("ew", 3), ("us", 0),
+    ("rs", 0, 3, 1), ("rs", 1, 3, 1), ("us", 1), ("us", 2), ("us", 3), ("rs", 0, 1, 4),
+    ("rs", 1, 1, 4), ("rs", 0, 2, 2), ("rs", 1, 2, 2), ("rs", 0, 3, 2), ("rs", 1, 3, 2), ("re", 1),
+    ("ui", 0), ("rs", 0, 2, 3), ("rs", 1, 2, 3), ("rs", 0, 3, 3), ("rs", 1, 3, 3), ("ui", 1),
+    ("rs", 0, 2, 4), ("rs", 1, 2, 4), ("rs", 0, 3, 4), ("rs", 1, 3, 4), ("ui", 2), ("re", 2),
+    ("re", 3), ("ui", 3),
+)
 
 
 def dot(a, b):
@@ -42,9 +105,9 @@
 def kernel(
     x_ref, q_ref, do_ref, doc_ref, gain_ref, w_ref, fl_ref, fm_ref, fmo_ref,
     dq_out, dx_out, dw_out, dg_out, mn_out, mo_out, fn_out,
-    X, XO, XT, Q, DO, WR, WB, PIN, POUT, PRAW, E, UOUT, UIN, DX, RB, SB, DW,
-    INV, CO, COS, SIN, BLO, BHI, KB, VB, KT, DKA, DVA, GC, DG,
-    F, FS, FSUM, XR, YS, YR, MW, FN, M0, M1, MB, MSB, R1, R2, MN, MO,
+    X, XO, XT, Q, DO, WR, WB, PIN, POUT, PRAW, E, UOUT, UIN, RB, SB,
+    INV, CO, COS, SIN, BLO, BHI, KB, VB, KT, DKA, DVA, GC, GT,
+    F, FS, FSUM, XR, YS, YR, MW, M01, MB, MSB, R1, R2, PK, DOC, GAIN,
     ag_s, ag_r, rs_s, rs_r, x_s, x_r, p_s, p_r, e_s, e_r, u_s, u_r, o_s, o_r, l_s,
 ):
     f = lax.axis_index("fsdp")
@@ -79,15 +142,16 @@
     ld_q = pltpu.make_async_copy(q_ref, Q, l_s.at[3])
     ld_do = pltpu.make_async_copy(do_ref, DO, l_s.at[4])
     ld_f = pltpu.make_async_copy(fl_ref.at[0], F, l_s.at[5])
-    ld_m0 = pltpu.make_async_copy(fm_ref, M0, l_s.at[6])
-    ld_m1 = pltpu.make_async_copy(fmo_ref, M1, l_s.at[7])
-    for c in (ld_w, ld_x, ld_xo, ld_f, ld_m0, ld_m1, ld_q, ld_do):
+    ld_m0 = pltpu.make_async_copy(fm_ref, M01.at[0:64], l_s.at[6])
+    ld_m1 = pltpu.make_async_copy(fmo_ref, M01.at[64:128], l_s.at[7])
+    ld_doc = pltpu.make_async_copy(doc_ref, DOC, l_s.at[8])
+    ld_gain = pltpu.make_async_copy(gain_ref, GAIN, l_s.at[9])
+    for c in (ld_w, ld_gain, ld_x, ld_xo, ld_f, ld_m0, ld_m1, ld_doc, ld_q, ld_do):
         c.start()
 
     barrier = pltpu.get_barrier_semaphore()
     for d in (left, right, partner, sibling, across, *xpeer):
         pl.semaphore_signal(barrier, inc=1, device_id=d, device_id_type=pl.DeviceIdType.MESH)
-    pl.semaphore_wait(barrier, 8)
 
     def x_copy(j):
         return remote(
@@ -96,9 +160,6 @@
             x_s.at[j], x_r.at[j], partner,
         )
 
-    for j in range(PIECES):
-        x_copy(j).start()
-
     def ring_at(dist):
         return lax.rem(z + dist + 2 * RING, RING)
 
@@ -117,11 +178,14 @@
     def ag_recv(d, g, s):
         return ag_copy(d, g, s, ring_at(-s if d == 0 else s))
 
-    def ag_step(g, s):
+    def ag_step(d, g, s):
+        ag_recv(d, g, s).wait_recv()
+        if s < 4:
+            ag_send(d, g, s + 1).start()
+
+    def ag_own(g):
         for d in (0, 1):
-            ag_recv(d, g, s).wait_recv()
-            if s < 4:
-                ag_send(d, g, s + 1).start()
+            ag_send(d, g, 1).start()
 
     eye = lax.broadcasted_iota(jnp.int32, (TOK, TOK), 0) == lax.broadcasted_iota(jnp.int32, (TOK, TOK), 1)
 
@@ -129,7 +193,8 @@
         square = jnp.where(eye, jnp.broadcast_to(row, (TOK, TOK)), 0.0).astype(bf16)
         return dot(square, jnp.ones((TOK, HD), bf16))
 
-    gain_row = gain_ref[...].astype(f32)
+    ld_gain.wait()
+    gain_row = GAIN[...].astype(f32)
     gain = column(gain_row)
     GC[...] = gain
     ld_w.wait()
@@ -141,12 +206,16 @@
             WR[:, 512 + g * HD : 512 + (g + 1) * HD].astype(f32) * gain
         ).astype(bf16)
 
-    for g in (0, 1):
-        scale_w(g)
-        for d in (0, 1):
-            ag_send(d, g, 1).start()
-    for g in (2, 3):
-        scale_w(g)
+    scale_w(0)
+    pl.semaphore_wait(barrier, 8)
+    x_copy(0).start()
+    ag_own(0)
+    for j in range(1, PIECES):
+        x_copy(j).start()
+    scale_w(1)
+    ag_own(1)
+    scale_w(2)
+    scale_w(3)
 
     rows_k = pl.ds(al(core * 128, 128), 128)
     rows_o = pl.ds(al((1 - core) * 128, 128), 128)
@@ -191,7 +260,7 @@
         ld_f.wait()
         ld_m0.wait()
         ld_m1.wait()
-        MB[...] = jnp.concatenate([M0[...], M1[...]], axis=1)
+        MB[...] = M01[...].T
         o_frag.start()
         o_state.start()
 
@@ -231,18 +300,17 @@
         R1[...] = jnp.where(core == 0, pack_1, pack_0)
         o_pack.start()
         keep = jnp.where(core == 0, pack_0, pack_1)
-        MN[rows_k, :] = keep[:, 0:64]
-        MO[rows_k, :] = keep[:, 64:128]
+        PK[rows_k, :] = keep
 
     def outer_5():
         o_back_y_in.wait_recv()
         for j in range(3):
             o_back_x(j).start()
         o_pack.wait_recv()
-        MN[rows_o, :] = R2[:, 0:64]
-        MO[rows_o, :] = R2[:, 64:128]
-        st_mn.start()
-        st_mo.start()
+        PK[rows_o, :] = R2[...]
+        both = PK[...].T
+        mn_out[...] = both[0:64]
+        mo_out[...] = both[64:128]
 
     def outer_6():
         for j in range(3):
@@ -251,15 +319,11 @@
 
     def outer_7():
         o_back_s_in.wait_recv()
-        FN[...] = (mixing * F[...].astype(f32) + (1.0 - mixing) * MW[...].astype(f32)).astype(bf16)
-        st_fn.start()
-
-    st_mn = pltpu.make_async_copy(MN, mn_out, l_s.at[8])
-    st_mo = pltpu.make_async_copy(MO, mo_out, l_s.at[9])
-    st_fn = pltpu.make_async_copy(FN, fn_out.at[0], l_s.at[10])
+        fn_out[0] = (mixing * F[...].astype(f32) + (1.0 - mixing) * MW[...].astype(f32)).astype(bf16)
 
     def tables():
-        doc_row = doc_ref[...].astype(f32)
+        ld_doc.wait()
+        doc_row = DOC[...].astype(f32)
         doc = column(doc_row)
         doc2 = jnp.concatenate([doc, doc], axis=1)
         row = jnp.broadcast_to(doc_row, (TOK, TOK))
@@ -295,9 +359,11 @@
     def p_copy(g):
         return remote(POUT.at[g], PIN.at[g], p_s.at[g], p_r.at[g], partner)
 
-    def project(g):
+    def project_partner(g):
         POUT[g] = dot(X[TOK : 2 * TOK, :], WB[g]).astype(bf16)
         p_copy(g).start()
+
+    def project_own(g):
         PRAW[g] = dot(X[0:TOK, :], WB[g])
 
     def e_copy(g):
@@ -353,22 +419,18 @@
         dq, dk, dv = attend(
             KB[...], VB[...], KT[...], both(Q, high_rows), both(DO, high_rows), BHI[...]
         )
-        Q[high_rows, ca] = dq[0:128]
-        Q[high_rows, cb] = dq[128:256]
+        dq_out[high_rows, ca] = dq[0:128]
+        dq_out[high_rows, cb] = dq[128:256]
         DKA[...] += dk
         DVA[...] += dv
         dq, dk, dv = attend(
             KB[low_rows, :], VB[low_rows, :], KT[:, low_rows],
             both(Q, low_rows), both(DO, low_rows), BLO[...],
         )
-        Q[low_rows, ca] = dq[0:128]
-        Q[low_rows, cb] = dq[128:256]
+        dq_out[low_rows, ca] = dq[0:128]
+        dq_out[low_rows, cb] = dq[128:256]
         DKA[low_rows, :] += dk
         DVA[low_rows, :] += dv
-
-    def dq_store(g):
-        cols = pl.ds(al(g * 1024, 1024), 1024)
-        return pltpu.make_async_copy(Q.at[:, cols], dq_out.at[:, cols], l_s.at[11 + g])
 
     def rs_copy(d, g, s):
         i = ag_sem(d, g, s)
@@ -382,24 +444,23 @@
     def term(owner, g):
         return dot(XT[pl.ds(al(owner * TOK, TOK), TOK), :], E[g])
 
-    def rs_step(g, s):
-        for d in (0, 1):
-            owner = ring_at(5 - s if d == 0 else s - 5)
-            i = ag_sem(d, g, s)
-            if s == 1:
-                start = al(owner * TOK + d * 128, 128)
-                SB[i, d * 128 : d * 128 + 128] = dot(XT[pl.ds(start, 128), :], E[g]).astype(bf16)
+    def rs_step(d, g, s):
+        owner = ring_at(5 - s if d == 0 else s - 5)
+        i = ag_sem(d, g, s)
+        if s == 1:
+            start = al(owner * TOK + d * 128, 128)
+            SB[i, d * 128 : d * 128 + 128] = dot(XT[pl.ds(start, 128), :], E[g]).astype(bf16)
+        else:
+            total = term(owner, g)
+            rs_copy(d, g, s - 1).wait_recv()
+            if s == 2:
+                came = slice(d * 128, d * 128 + 128)
+                rest = slice((1 - d) * 128, (1 - d) * 128 + 128)
+                SB[i, came] = (total[came] + RB[i - 1, came].astype(f32)).astype(bf16)
+                SB[i, rest] = total[rest].astype(bf16)
             else:
-                total = term(owner, g)
-                rs_copy(d, g, s - 1).wait_recv()
-                if s == 2:
-                    came = slice(d * 128, d * 128 + 128)
-                    rest = slice((1 - d) * 128, (1 - d) * 128 + 128)
-                    SB[i, came] = (total[came] + RB[i - 1, came].astype(f32)).astype(bf16)
-                    SB[i, rest] = total[rest].astype(bf16)
-                else:
-                    SB[i] = (total + RB[i - 1].astype(f32)).astype(bf16)
-            rs_copy(d, g, s).start()
+                SB[i] = (total + RB[i - 1].astype(f32)).astype(bf16)
+        rs_copy(d, g, s).start()
 
     def rs_end(g):
         total = term(z, g)
@@ -409,10 +470,10 @@
         ck, cv = g * HD, 512 + g * HD
         wide_gain = GC[...]
         tk, tv = total[:, 0:HD], total[:, HD : 2 * HD]
-        DW[:, ck : ck + HD] = tk * wide_gain
-        DW[:, cv : cv + HD] = tv * wide_gain
+        dw_out[0, :, ck : ck + HD] = tk * wide_gain
+        dw_out[0, :, cv : cv + HD] = tv * wide_gain
         part = tk * WR[:, ck : ck + HD].astype(f32) + tv * WR[:, cv : cv + HD].astype(f32)
-        return jnp.sum(part, axis=1, keepdims=True)
+        GT[...] += jnp.broadcast_to(jnp.sum(part, axis=1, keepdims=True), (TOK, HD))
 
     def u_copy(j):
         return remote(UOUT.at[j], UIN.at[j], u_s.at[j], u_r.at[j], partner)
@@ -424,12 +485,6 @@
             total = total + dot_nt(E[g, first : first + TOK], WB[g, rows])
         return total
 
-    def dx_store(part, j):
-        start = al((h if part == 0 else 1 - h) * HALF + j * PIECE, PIECE)
-        return pltpu.make_async_copy(
-            DX.at[part * PIECES + j], dx_out.at[:, pl.ds(start, PIECE)], l_s.at[15 + part * PIECES + j]
-        )
-
     def send_upstream(j):
         UOUT[j] = upstream(TOK, j).astype(bf16)
         u_copy(j).start()
@@ -439,121 +494,65 @@
         x = X[0:TOK, cols] if part == 0 else XO[:, cols]
         c = CO[...]
         c = jnp.concatenate([c] * (PIECE // HD), axis=1)
-        DX[part * PIECES + j] = (u - x.astype(f32) * c).astype(bf16)
-        dx_store(part, j).start()
-
-    outer_1()
-    tables()
-    ag_step(0, 1)
-    outer_2()
-    ag_step(1, 1)
-    inverse()
-    ag_step(0, 2)
-    transpose_x(0, 0)
-    transpose_x(0, 1)
-    ag_step(1, 2)
-    transpose_x(0, 2)
-    transpose_x(0, 3)
-    outer_3()
-    ag_step(0, 3)
-    x_copy(0).wait_recv()
-    transpose_x(1, 0)
-    ag_step(1, 3)
-    for g in (2, 3):
-        for d in (0, 1):
-            ag_send(d, g, 1).start()
-    outer_4()
-    x_copy(1).wait_recv()
-    transpose_x(1, 1)
-    ag_step(0, 4)
-    ag_step(1, 4)
-    outer_5()
-    x_copy(2).wait_recv()
-    transpose_x(1, 2)
-    x_copy(3).wait_recv()
-    project(0)
-    project(1)
-    transpose_x(1, 3)
-    ld_q.wait()
-    ld_do.wait()
-
-    def attention(base, hook):
-        def step(n, _):
-            g = base + lax.div(n, PAIRS)
-            part = lax.rem(n, PAIRS)
-
-            @pl.when(part == 0)
-            def _():
-                group_start(g)
-
-            head_pair((base * PAIRS + n) * 2 * HD)
-
-            @pl.when(part == PAIRS - 1)
-            def _():
-                group_end(g)
-                dq_store(g).start()
-
-            hook(n)
-            return 0
-
-        lax.fori_loop(0, 2 * PAIRS, step, 0)
-
-    def ag_hook(n):
-        g, hop = 2 + lax.rem(n, 2), lax.div(n, 2)
-        for s in (1, 2, 3, 4):
-
-            @pl.when(hop == s - 1)
-            def _(s=s):
-                ag_step(g, s)
-
-    def rs_hook(n):
-        g, hop = lax.rem(n, 2), lax.div(n, 2)
-        for s in (1, 2, 3, 4):
-
-            @pl.when(hop == s - 1)
-            def _(s=s):
-                rs_step(g, s)
-
-    attention(0, ag_hook)
-    outer_6()
-    project(2)
-    project(3)
-    for g in (0, 1):
-        e_copy(g).wait_recv()
-    attention(2, rs_hook)
-    outer_7()
-    e_copy(2).wait_recv()
-    rs_step(2, 1)
-    e_copy(3).wait_recv()
-    rs_step(3, 1)
-    CO[...] = CO[...] * INV[...] * INV[...] * (1.0 / WIDE)
-    for j in range(PIECES):
-        send_upstream(j)
-    rs_step(2, 2)
-    rs_step(3, 2)
-    gain_total = rs_end(0)
-    finish(0, 0, upstream(0, 0))
-    rs_step(2, 3)
-    rs_step(3, 3)
-    gain_total = gain_total + rs_end(1)
-    finish(0, 1, upstream(0, 1))
-    rs_step(2, 4)
-    rs_step(3, 4)
-    finish(0, 2, upstream(0, 2))
-    finish(0, 3, upstream(0, 3))
-    for j in range(PIECES - 1):
+        start = al((h if part == 0 else 1 - h) * HALF + j * PIECE, PIECE)
+        dx_out[:, pl.ds(start, PIECE)] = (u - x.astype(f32) * c).astype(bf16)
+
+    def outer(k):
+        (outer_1, outer_2, outer_3, outer_4, outer_5, outer_6, outer_7)[k - 1]()
+
+    def x_transpose(who, j):
+        if who == 1 and j < PIECES - 1:
+            x_copy(j).wait_recv()
+        transpose_x(who, j)
+
+    def start_group(g):
+        if g == 0:
+            ld_q.wait()
+            ld_do.wait()
+        group_start(g)
+
+    def end_group(g):
+        group_end(g)
+        if g == GROUPS - 1:
+            CO[...] = CO[...] * INV[...] * INV[...] * (1.0 / WIDE)
+
+    def first_projection(g):
+        if g == 0:
+            x_copy(PIECES - 1).wait_recv()
+        project_partner(g)
+
+    def upstream_in(j):
         u_copy(j).wait_recv()
         finish(1, j, UIN[j].astype(f32))
-    gain_total = gain_total + rs_end(2)
-    gain_total = gain_total + rs_end(3)
-    st_dw = pltpu.make_async_copy(DW, dw_out.at[0], l_s.at[23])
-    st_dw.start()
-    spread = jnp.where(eye, jnp.broadcast_to(gain_total, (TOK, TOK)), 0.0)
-    DG[...] = jnp.sum(spread, axis=0, keepdims=True)
-    st_dg = pltpu.make_async_copy(DG, dg_out, l_s.at[24])
-    st_dg.start()
-    u_copy(PIECES - 1).wait_recv()
-    finish(1, PIECES - 1, UIN[PIECES - 1].astype(f32))
+
+    acts = dict(
+        ag=ag_step, own=ag_own, tab=tables, inv=inverse, tr=x_transpose, pp=first_projection, po=project_own,
+        gs=start_group, ge=end_group, rs=rs_step, ew=lambda g: e_copy(g).wait_recv(), re=rs_end, us=send_upstream,
+        uo=lambda j: finish(0, j, upstream(0, j)), ui=upstream_in, o=outer,
+    )
+
+    def play(items):
+        for name, *numbers in items:
+            acts[name](*numbers)
+
+    GT[...] = jnp.zeros_like(GT)
+    play(BEFORE)
+
+    def step(n, _):
+        for k, items in enumerate(DURING):
+            if items:
+
+                @pl.when(n == k)
+                def _(items=items):
+                    play(items)
+
+        head_pair(n * 2 * HD)
+        return 0
+
+    lax.fori_loop(0, GROUPS * PAIRS, step, 0)
+    play(AFTER)
+    spread = jnp.where(eye, jnp.concatenate([GT[...], GT[...]], axis=1), 0.0)
+    dg_out[...] = jnp.sum(spread, axis=0, keepdims=True)
 
     for j in range(PIECES):
         x_copy(j).wait_send()
@@ -566,7 +565,6 @@
             for d in (0, 1):
                 ag_send(d, g, s).wait_send()
                 rs_copy(d, g, s).wait_send()
-        dq_store(g).wait()
         return 0
 
     lax.fori_loop(0, GROUPS, drain, 0)
@@ -575,16 +573,22 @@
     for j in range(3):
         o_x(j).wait_send()
         o_back_x(j).wait_send()
-    for part in (0, 1):
-        for j in range(PIECES):
-            dx_store(part, j).wait()
-    for c in (st_mn, st_mo, st_fn, st_dw, st_dg):
+
+
+def store(*refs):
+    n = len(refs) // 2
+    sems = refs[-1]
+    copies = [pltpu.make_async_copy(refs[i], refs[n + i], sems.at[i]) for i in range(n)]
+    for c in copies:
+        c.start()
+    for c in copies:
         c.wait()
 
 
 def on_device(x, q, do, doc, gain, w, fl, fm, fmo):
     sds = jax.ShapeDtypeStruct
-    hbm = pl.BlockSpec(memory_space=pl.ANY)
+    hbm = pl.BlockSpec(memory_space=pltpu.HBM)
+    anywhere = pl.BlockSpec(memory_space=pl.ANY)
     vmem = pl.BlockSpec(memory_space=pltpu.VMEM)
 
     def v(shape, t):
@@ -605,10 +609,8 @@
         v((GROUPS, 2 * TOK, 256), bf16),
         v((PIECES, TOK, PIECE), bf16),
         v((PIECES, TOK, PIECE), bf16),
-        v((2 * PIECES, TOK, PIECE), bf16),
         v((32, TOK, 256), bf16),
         v((32, TOK, 256), bf16),
-        v((TOK, 1024), f32),
         v((TOK, HD), f32),
         v((TOK, HD), f32),
         v((TOK, HD), f32),
@@ -621,7 +623,7 @@
         v((TOK, HD), f32),
         v((TOK, HD), f32),
         v((TOK, HD), f32),
-        v((1, TOK), f32),
+        v((TOK, HD), f32),
         v((256, 1024), bf16),
         v((128, 1024), bf16),
         v((128, 1024), bf16),
@@ -629,39 +631,49 @@
         v((128, 128), bf16),
         v((128, 128), bf16),
         v((256, 1024), bf16),
-        v((256, 1024), bf16),
-        v((256, 64), f32),
-        v((256, 64), f32),
+        v((128, 256), f32),
         v((256, 128), f32),
         v((128, 128), f32),
         v((128, 128), f32),
         v((128, 128), f32),
-        v((256, 64), f32),
-        v((256, 64), f32),
+        v((256, 128), f32),
+        v((1, 256), jnp.int32),
+        v((1, 256), bf16),
         dma((32,)), dma((32,)), dma((32,)), dma((32,)),
         dma((4,)), dma((4,)), dma((4,)), dma((4,)),
         dma((4,)), dma((4,)), dma((4,)), dma((4,)),
-        dma((12,)), dma((12,)), dma((25,)),
+        dma((12,)), dma((12,)), dma((10,)),
     ]
-    return pl.pallas_call(
+    shapes = (
+        sds((TOK, WIDE), bf16),
+        sds((TOK, WIDE), bf16),
+        sds((1, 256, 1024), f32),
+        sds((1, 256), f32),
+        sds((64, 256), f32),
+        sds((64, 256), f32),
+        sds((1, 256, 1024), bf16),
+    )
+    results = pl.pallas_call(
         kernel,
-        out_shape=(
-            sds((TOK, WIDE), bf16),
-            sds((TOK, WIDE), bf16),
-            sds((1, 256, 1024), f32),
-            sds((1, 256), f32),
-            sds((256, 64), f32),
-            sds((256, 64), f32),
-            sds((1, 256, 1024), bf16),
-        ),
-        in_specs=[hbm, hbm, hbm, vmem, vmem, hbm, hbm, hbm, hbm],
-        out_specs=(hbm,) * 7,
+        out_shape=tuple(pltpu.VMEM(a.shape, a.dtype) for a in shapes),
+        in_specs=[hbm] * 9,
+        out_specs=(vmem,) * 7,
         scratch_shapes=scratch,
         compiler_params=pltpu.CompilerParams(
-            collective_id=0, has_side_effects=True, vmem_limit_bytes=48 * 2**20
+            collective_id=0, has_side_effects=True, vmem_limit_bytes=VMEM_LIMIT
         ),
         name="step",
-    )(x, q, do, doc, gain, w, fl, fm, fmo)
+    )(*(pltpu.with_memory_space_constraint(a, pltpu.HBM) for a in (x, q, do, doc, gain, w, fl, fm.T, fmo.T)))
+    dq, dx, dw, dg, mn, mo, fn = pl.pallas_call(
+        store,
+        out_shape=shapes,
+        in_specs=[anywhere] * 7,
+        out_specs=(hbm,) * 7,
+        scratch_shapes=[dma((7,))],
+        compiler_params=pltpu.CompilerParams(vmem_limit_bytes=2**20),
+        name="store",
+    )(*results)
+    return dq, dx, dw, dg, mn.T, mo.T, fn
 
 
 def solution(mesh):

time: 129 us -> 102 us (0.79)
  local copies, waits for them, and re-layouts: 15.1 us -> 0 us
  Pallas kernels: 113 us -> 101 us
    unnamed x23 -> x0, local copies, waits for them, and re-layouts: 12.7 us -> none
    pallas_call x1 -> x2, Pallas kernels: 113 us -> 101 us  [the longest x1 98.8 us: on_device(): pl.pallas_call(kernel, out_shape=tuple((pltpu.VMEM(a.shape, a.dtype) for...]
    pallas_call x2 -> x0, local copies, waits for them, and re-layouts: 2.33 us -> none  [on_device(): pl.pallas_call(kernel, out_shape=(sds((TOK, WIDE), bf16), sds((TOK, WIDE)...]
where the time goes in v2:
time: 102 us
  Pallas kernels  101 us (99%)
    pallas_call x1, Pallas kernels, on_device(): pl.pallas_call(kernel, out_shape=tuple((pltpu.VMEM(a.shape, a.dtype) for...  98.8 us
    pallas_call x1, Pallas kernels, on_device(): pl.pallas_call(store, out_shape=shapes, in_specs=[anywhere] * 7, out_spec...  2.6 us

profile of v2, /device:TPU:6, one launch (start us, length us, event | category | flops | bytes accessed | tf_op | source)
XLA Modules:
  0.0 102.2 jit_solution(11141504075366653096)
XLA Ops:
  0.6 98.8 %step.1 = (bf16[256,4096]{1,0:T(8,128)(2,1)S(1)}, bf16[256,4096]{1,0:T(8,128)(2,1)S(1)}, f32[1,256,1024]{2,1,0:T(8,128)S(1)}, f32[1,256]{1,0:T(1,128)S(1)}, f32[...) custom-call(bf16[256,4096]{1,0:T(8,128)(2,1)} %x_ref.1, bf16[256,4096]{1,0:T(8,128)(2,1)} %q_ref.1, ...), custom_call_target="tpu_custom_call" | custom-call | tf_op jit(solution)/shard_map/step/pallas_call | solution.py:656
  99.5 2.6 %store.1 = (bf16[256,4096]{1,0:T(8,128)(2,1)}, bf16[256,4096]{1,0:T(8,128)(2,1)}, f32[1,256,1024]{2,1,0:T(8,128)}, f32[1,256]{1,0:T(1,128)}, f32[64,256]{1,0:T(8...) custom-call(bf16[256,4096]{1,0:T(8,128)(2,1)S(1)} %get-tuple-element.21.refs_0_, ...), custom_call_target="tpu_custom_call" | custom-call | tf_op jit(solution)/shard_map/store/pallas_call | solution.py:667

commit v3 on v2

--- a/solution.py
+++ b/solution.py
@@ -18,7 +18,7 @@
 WIDE = 4096
 HALF = 2048
 GROUPS = 4
-PAIRS = 4
+QUAD = 512
 HD = 128
 RING = 8
 SCALE = HD ** (-0.5)
@@ -28,69 +28,64 @@
 
 f32 = jnp.float32
 bf16 = jnp.bfloat16
-VMEM_LIMIT = 40 * 2**20
+VMEM_LIMIT = 44 * 2**20
 NT = (((1,), (1,)), ((), ()))
 
 
 BEFORE = (
-    ("inv",), ("tab",), ("tr", 0, 0), ("tr", 0, 1), ("tr", 0, 2), ("tr", 0, 3), ("o", 1), ("o", 2),
-    ("ag", 0, 0, 1), ("ag", 1, 0, 1), ("tr", 1, 0), ("ag", 0, 1, 1), ("ag", 1, 1, 1), ("ag", 0, 0, 2),
-    ("ag", 1, 0, 2), ("own", 2), ("o", 3), ("tr", 1, 1), ("ag", 0, 1, 2), ("ag", 1, 1, 2),
-    ("ag", 0, 0, 3), ("ag", 1, 0, 3), ("tr", 1, 2), ("ag", 0, 2, 1), ("ag", 1, 2, 1), ("own", 3),
-    ("ag", 0, 1, 3), ("ag", 1, 1, 3), ("ag", 0, 0, 4), ("ag", 1, 0, 4), ("po", 0), ("pp", 0),
-    ("tr", 1, 3), ("o", 4), ("ag", 0, 2, 2), ("ag", 1, 2, 2), ("ag", 0, 3, 1), ("ag", 1, 3, 1),
+    ("inv",), ("tab",), ("tr", 0, 0), ("tr", 0, 1), ("tr", 0, 2), ("tr", 0, 3), ("o", 1),
+    ("ag", 0, 0, 0, 1), ("ag", 1, 0, 1, 1), ("ag", 0, 0, 1, 1), ("ag", 1, 0, 0, 1), ("o", 2),
+    ("ag", 0, 1, 0, 1), ("ag", 1, 1, 1, 1), ("tr", 1, 0), ("ag", 0, 1, 1, 1), ("ag", 1, 1, 0, 1),
+    ("ag", 0, 0, 0, 2), ("ag", 1, 0, 1, 2), ("ag", 0, 0, 1, 2), ("ag", 1, 0, 0, 2), ("o", 3),
+    ("ag", 0, 1, 0, 2), ("ag", 1, 1, 1, 2), ("own", 2), ("tr", 1, 1), ("ag", 0, 1, 1, 2),
+    ("ag", 1, 1, 0, 2), ("ag", 0, 0, 0, 3), ("ag", 1, 0, 1, 3), ("ag", 0, 0, 1, 3), ("ag", 1, 0, 0, 3),
+    ("ag", 0, 1, 0, 3), ("ag", 1, 1, 1, 3), ("own", 3), ("tr", 1, 2), ("ag", 0, 2, 0, 1),
+    ("ag", 1, 2, 1, 1), ("ag", 0, 2, 1, 1), ("ag", 1, 2, 0, 1), ("ag", 0, 1, 1, 3), ("ag", 1, 1, 0, 3),
+    ("ag", 0, 0, 0, 4), ("ag", 1, 0, 1, 4), ("po", 0), ("pp", 0), ("ag", 0, 1, 0, 4),
+    ("ag", 1, 1, 1, 4), ("pp", 1), ("po", 1), ("tr", 1, 3), ("o", 4), ("ag", 0, 3, 0, 1),
+    ("ag", 1, 3, 1, 1), ("ag", 0, 3, 1, 1), ("ag", 1, 3, 0, 1), ("ag", 0, 2, 0, 2), ("ag", 1, 2, 1, 2),
     ("gs", 0),
 )
 DURING = (
     (),
     (
-        ("ag", 0, 1, 4), ("ag", 1, 1, 4), ("pp", 1), ("po", 1),
+        ("ag", 0, 2, 1, 2), ("ag", 1, 2, 0, 2),
+    ),
+    (
+        ("ag", 0, 3, 0, 2), ("ag", 1, 3, 1, 2), ("ge", 0), ("dq", 0), ("gs", 1), ("ag", 0, 3, 1, 2),
+        ("ag", 1, 3, 0, 2),
     ),
     (),
     (
-        ("ag", 0, 2, 3), ("ag", 1, 2, 3),
-    ),
-    (
-        ("ge", 0), ("o", 5), ("gs", 1),
-    ),
-    (
-        ("ag", 0, 3, 2), ("ag", 1, 3, 2),
-    ),
-    (
-        ("ag", 0, 2, 4), ("ag", 1, 2, 4), ("pp", 2), ("po", 2),
-    ),
-    (
-        ("ew", 0), ("rs", 0, 0, 1), ("rs", 1, 0, 1),
-    ),
-    (
-        ("ge", 1), ("ag", 0, 3, 3), ("ag", 1, 3, 3), ("o", 6), ("gs", 2), ("rs", 0, 0, 2), ("rs", 1, 0, 2),
-    ),
-    (
-        ("ag", 0, 3, 4), ("ag", 1, 3, 4), ("pp", 3), ("po", 3),
-    ),
-    (
-        ("ew", 1), ("rs", 0, 1, 1), ("rs", 1, 1, 1),
-    ),
-    (
-        ("rs", 0, 0, 3), ("rs", 1, 0, 3),
-    ),
-    (
-        ("ge", 2), ("gs", 3), ("rs", 0, 1, 2), ("rs", 1, 1, 2),
+        ("ag", 0, 2, 0, 3), ("ag", 1, 2, 1, 3), ("ge", 1), ("dq", 1), ("ag", 0, 2, 1, 3),
+        ("ag", 1, 2, 0, 3), ("dq", 2), ("dq", 3), ("o", 5), ("ag", 0, 3, 0, 3), ("ag", 1, 3, 1, 3),
+        ("ew", 0), ("rs", 0, 0, 1, 1), ("rs", 1, 0, 0, 1), ("rs", 0, 0, 0, 1), ("rs", 1, 0, 1, 1),
+        ("ag", 0, 3, 1, 3), ("ag", 1, 3, 0, 3), ("ag", 0, 2, 0, 4), ("ag", 1, 2, 1, 4), ("pp", 2),
+        ("po", 2), ("ew", 1), ("rs", 0, 1, 1, 1), ("rs", 1, 1, 0, 1), ("rs", 0, 1, 0, 1),
+        ("rs", 1, 1, 1, 1), ("ag", 0, 3, 0, 4), ("ag", 1, 3, 1, 4), ("pp", 3), ("po", 3),
+        ("rs", 0, 0, 1, 2), ("rs", 1, 0, 0, 2), ("o", 6), ("rs", 0, 0, 0, 2), ("rs", 1, 0, 1, 2),
+        ("gs", 2), ("rs", 0, 1, 1, 2), ("rs", 1, 1, 0, 2),
     ),
     (),
+    (
+        ("rs", 0, 1, 0, 2), ("rs", 1, 1, 1, 2), ("ge", 2), ("gs", 3), ("rs", 0, 0, 1, 3),
+        ("rs", 1, 0, 0, 3),
+    ),
     (),
-    (
-        ("rs", 0, 0, 4), ("rs", 1, 0, 4),
-    ),
 )
 AFTER = (
-    ("ew", 2), ("ge", 3), ("rs", 0, 1, 3), ("rs", 1, 1, 3), ("rs", 0, 2, 1), ("rs", 1, 2, 1),
-    ("uo", 0), ("uo", 1), ("uo", 2), ("uo", 3), ("o", 7), ("re", 0), ("ew", 3), ("us", 0),
-    ("rs", 0, 3, 1), ("rs", 1, 3, 1), ("us", 1), ("us", 2), ("us", 3), ("rs", 0, 1, 4),
-    ("rs", 1, 1, 4), ("rs", 0, 2, 2), ("rs", 1, 2, 2), ("rs", 0, 3, 2), ("rs", 1, 3, 2), ("re", 1),
-    ("ui", 0), ("rs", 0, 2, 3), ("rs", 1, 2, 3), ("rs", 0, 3, 3), ("rs", 1, 3, 3), ("ui", 1),
-    ("rs", 0, 2, 4), ("rs", 1, 2, 4), ("rs", 0, 3, 4), ("rs", 1, 3, 4), ("ui", 2), ("re", 2),
-    ("re", 3), ("ui", 3),
+    ("rs", 0, 0, 0, 3), ("rs", 1, 0, 1, 3), ("ge", 3), ("rs", 0, 1, 1, 3), ("rs", 1, 1, 0, 3),
+    ("uo", 0), ("uo", 1), ("uo", 2), ("rs", 0, 1, 0, 3), ("rs", 1, 1, 1, 3), ("uo", 3), ("ew", 2),
+    ("rs", 0, 2, 1, 1), ("rs", 1, 2, 0, 1), ("rs", 0, 2, 0, 1), ("rs", 1, 2, 1, 1), ("dq", 4),
+    ("dq", 5), ("dq", 6), ("rs", 0, 0, 0, 4), ("rs", 1, 0, 1, 4), ("dq", 7), ("ew", 3), ("us", 0),
+    ("rs", 0, 3, 1, 1), ("rs", 1, 3, 0, 1), ("rs", 0, 3, 0, 1), ("rs", 1, 3, 1, 1), ("us", 1),
+    ("us", 2), ("us", 3), ("rs", 0, 1, 0, 4), ("rs", 1, 1, 1, 4), ("o", 7), ("rs", 0, 2, 1, 2),
+    ("rs", 1, 2, 0, 2), ("rs", 0, 2, 0, 2), ("rs", 1, 2, 1, 2), ("re", 0), ("rs", 0, 3, 1, 2),
+    ("rs", 1, 3, 0, 2), ("ui", 0), ("rs", 0, 3, 0, 2), ("rs", 1, 3, 1, 2), ("re", 1),
+    ("rs", 0, 2, 1, 3), ("rs", 1, 2, 0, 3), ("rs", 0, 2, 0, 3), ("rs", 1, 2, 1, 3), ("ui", 1),
+    ("rs", 0, 3, 1, 3), ("rs", 1, 3, 0, 3), ("rs", 0, 3, 0, 3), ("rs", 1, 3, 1, 3), ("rs", 0, 2, 0, 4),
+    ("rs", 1, 2, 1, 4), ("ui", 2), ("rs", 0, 3, 0, 4), ("rs", 1, 3, 1, 4), ("re", 2), ("ui", 3),
+    ("re", 3),
 )
 
 
@@ -106,7 +101,7 @@
     x_ref, q_ref, do_ref, doc_ref, gain_ref, w_ref, fl_ref, fm_ref, fmo_ref,
     dq_out, dx_out, dw_out, dg_out, mn_out, mo_out, fn_out,
     X, XO, XT, Q, DO, WR, WB, PIN, POUT, PRAW, E, UOUT, UIN, RB, SB,
-    INV, CO, COS, SIN, BLO, BHI, KB, VB, KT, DKA, DVA, GC, GT,
+    INV, CO, COS, SIN, BLO, BHI, DSH, DSL, KB, VB, KT, DKA, DVA, GC, GT,
     F, FS, FSUM, XR, YS, YR, MW, M01, MB, MSB, R1, R2, PK, DOC, GAIN,
     ag_s, ag_r, rs_s, rs_r, x_s, x_r, p_s, p_r, e_s, e_r, u_s, u_r, o_s, o_r, l_s,
 ):
@@ -163,29 +158,32 @@
     def ring_at(dist):
         return lax.rem(z + dist + 2 * RING, RING)
 
-    def ag_sem(d, g, s):
-        return d * 16 + g * 4 + (s - 1)
-
-    def ag_copy(d, g, s, shard):
-        start, size = (shard * TOK, TOK) if s < 4 else (shard * TOK + d * 128, 128)
-        block = WB.at[g, pl.ds(al(start, 128), size)]
-        i = ag_sem(d, g, s)
+    def hops(d, c):
+        return RING // 2 if c == d else RING // 2 - 1
+
+    def ring_sem(d, g, c, s):
+        return ((d * GROUPS + g) * 2 + c) * 4 + s - 1
+
+    def ag_copy(d, g, c, s, shard):
+        block = WB.at[g, pl.ds(al(shard * TOK + c * 128, 128), 128)]
+        i = ring_sem(d, g, c, s)
         return remote(block, block, ag_s.at[i], ag_r.at[i], (right, left)[d])
 
-    def ag_send(d, g, s):
-        return ag_copy(d, g, s, ring_at((1 - s) if d == 0 else (s - 1)))
-
-    def ag_recv(d, g, s):
-        return ag_copy(d, g, s, ring_at(-s if d == 0 else s))
-
-    def ag_step(d, g, s):
-        ag_recv(d, g, s).wait_recv()
-        if s < 4:
-            ag_send(d, g, s + 1).start()
+    def ag_send(d, g, c, s):
+        return ag_copy(d, g, c, s, ring_at((1 - s) if d == 0 else (s - 1)))
+
+    def ag_recv(d, g, c, s):
+        return ag_copy(d, g, c, s, ring_at(-s if d == 0 else s))
+
+    def ag_step(d, g, c, s):
+        ag_recv(d, g, c, s).wait_recv()
+        if s < hops(d, c):
+            ag_send(d, g, c, s + 1).start()
 
     def ag_own(g):
-        for d in (0, 1):
-            ag_send(d, g, 1).start()
+        for c in (0, 1):
+            for d in (0, 1):
+                ag_send(d, g, c ^ d, 1).start()
 
     eye = lax.broadcasted_iota(jnp.int32, (TOK, TOK), 0) == lax.broadcasted_iota(jnp.int32, (TOK, TOK), 1)
 
@@ -208,10 +206,9 @@
 
     scale_w(0)
     pl.semaphore_wait(barrier, 8)
-    x_copy(0).start()
+    for j in range(PIECES):
+        x_copy(j).start()
     ag_own(0)
-    for j in range(1, PIECES):
-        x_copy(j).start()
     scale_w(1)
     ag_own(1)
     scale_w(2)
@@ -338,8 +335,8 @@
         u = lax.broadcasted_iota(jnp.int32, (TOK, TOK), 0)
         t = lax.broadcasted_iota(jnp.int32, (TOK, TOK), 1)
         bias = jnp.where((u <= t) & (row == doc2), 0.0, masked_score)
-        BLO[...] = jnp.concatenate([bias[0:128, 0:128], bias[0:128, 0:128]], axis=1)
-        BHI[...] = jnp.concatenate([bias[:, 128:256], bias[:, 128:256]], axis=1)
+        BLO[...] = jnp.concatenate([bias[0:128, 0:128]] * 4, axis=1)
+        BHI[...] = jnp.concatenate([bias[:, 128:256]] * 4, axis=1)
 
     def inverse():
         ld_x.wait()
@@ -378,7 +375,7 @@
         k = k * COS[...] + pltpu.roll(k, 64, 1) * SIN[...]
         kb = k.astype(bf16)
         KB[...] = kb
-        KT[...] = kb.T
+        KT[g] = kb.T
         VB[...] = (raw[:, HD : 2 * HD] * inv).astype(bf16)
         DKA[...] = jnp.zeros_like(DKA)
         DVA[...] = jnp.zeros_like(DVA)
@@ -396,77 +393,69 @@
         part = ek.astype(f32) * raw[:, 0:HD] + ev.astype(f32) * raw[:, HD : 2 * HD]
         CO[...] += jnp.broadcast_to(jnp.sum(part, axis=1, keepdims=True), (TOK, HD))
 
-    def attend(kb, vb, kt, qc, dc, bias):
-        s = dot_nt(kb, qc) + bias
-        w = dot_nt(vb, dc)
+    low_rows, high_rows = slice(0, 128), slice(128, 256)
+
+    def softmax(s, w):
         top = jnp.max(s, axis=0, keepdims=True)
         e = jnp.exp2((s - top) * EXP2_SCALE)
         p = e * (1.0 / jnp.sum(e, axis=0, keepdims=True))
         pw = p * w
         delta = jnp.sum(pw, axis=0, keepdims=True)
-        ds = (pw - p * delta).astype(bf16)
-        dq = (dot(kt, ds) * SCALE).T.astype(bf16)
-        return dq, dot(ds, qc), dot(p.astype(bf16), dc)
-
-    def head_pair(column_start):
-        ca = pl.ds(al(column_start, 256), HD)
-        cb = pl.ds(al(column_start + HD, HD), HD)
-        low_rows, high_rows = slice(0, 128), slice(128, 256)
-
-        def both(ref, rows):
-            return jnp.concatenate([ref[rows, ca], ref[rows, cb]], axis=0)
-
-        dq, dk, dv = attend(
-            KB[...], VB[...], KT[...], both(Q, high_rows), both(DO, high_rows), BHI[...]
-        )
-        dq_out[high_rows, ca] = dq[0:128]
-        dq_out[high_rows, cb] = dq[128:256]
-        DKA[...] += dk
-        DVA[...] += dv
-        dq, dk, dv = attend(
-            KB[low_rows, :], VB[low_rows, :], KT[:, low_rows],
-            both(Q, low_rows), both(DO, low_rows), BLO[...],
-        )
-        dq_out[low_rows, ca] = dq[0:128]
-        dq_out[low_rows, cb] = dq[128:256]
-        DKA[low_rows, :] += dk
-        DVA[low_rows, :] += dv
-
-    def rs_copy(d, g, s):
-        i = ag_sem(d, g, s)
-        if s == 1:
-            rows = slice(d * 128, d * 128 + 128)
-            src, dst = SB.at[i, rows], RB.at[i, rows]
-        else:
-            src, dst = SB.at[i], RB.at[i]
-        return remote(src, dst, rs_s.at[i], rs_r.at[i], (right, left)[d])
-
-    def term(owner, g):
-        return dot(XT[pl.ds(al(owner * TOK, TOK), TOK), :], E[g])
-
-    def rs_step(d, g, s):
-        owner = ring_at(5 - s if d == 0 else s - 5)
-        i = ag_sem(d, g, s)
-        if s == 1:
-            start = al(owner * TOK + d * 128, 128)
-            SB[i, d * 128 : d * 128 + 128] = dot(XT[pl.ds(start, 128), :], E[g]).astype(bf16)
-        else:
-            total = term(owner, g)
-            rs_copy(d, g, s - 1).wait_recv()
-            if s == 2:
-                came = slice(d * 128, d * 128 + 128)
-                rest = slice((1 - d) * 128, (1 - d) * 128 + 128)
-                SB[i, came] = (total[came] + RB[i - 1, came].astype(f32)).astype(bf16)
-                SB[i, rest] = total[rest].astype(bf16)
-            else:
-                SB[i] = (total + RB[i - 1].astype(f32)).astype(bf16)
-        rs_copy(d, g, s).start()
+        return p.astype(bf16), (pw - p * delta).astype(bf16)
+
+    def heads(n):
+        def rows_of(ref, rows):
+            return jnp.concatenate(
+                [ref[rows, pl.ds(al(n * QUAD + i * HD, HD), HD)] for i in range(4)], axis=0
+            )
+
+        q_high, d_high = rows_of(Q, high_rows), rows_of(DO, high_rows)
+        q_low, d_low = rows_of(Q, low_rows), rows_of(DO, low_rows)
+        kb, vb = KB[...], VB[...]
+        s_high, w_high = dot_nt(kb, q_high) + BHI[...], dot_nt(vb, d_high)
+        s_low, w_low = dot_nt(kb[low_rows], q_low) + BLO[...], dot_nt(vb[low_rows], d_low)
+        p_high, ds_high = softmax(s_high, w_high)
+        p_low, ds_low = softmax(s_low, w_low)
+        DSH[n] = ds_high
+        DSL[n] = ds_low
+        DKA[...] += dot(ds_high, q_high)
+        DVA[...] += dot(p_high, d_high)
+        DKA[low_rows, :] += dot(ds_low, q_low)
+        DVA[low_rows, :] += dot(p_low, d_low)
+
+    def query_gradient(n):
+        g = n // 2
+        for rows, ds in ((high_rows, DSH[n]), (low_rows, DSL[n])):
+            kt = KT[g] if rows is high_rows else KT[g, :, 0:128]
+            dq = (dot(kt, ds) * SCALE).T.astype(bf16)
+            for i in range(4):
+                c = n * QUAD + i * HD
+                dq_out[rows, c : c + HD] = dq[i * 128 : (i + 1) * 128]
+
+    def rs_copy(d, g, c, s):
+        i = ring_sem(d, g, c, s)
+        return remote(SB.at[i], RB.at[i], rs_s.at[i], rs_r.at[i], (right, left)[d])
+
+    def rs_step(d, g, c, s):
+        far = hops(d, c) + 1 - s
+        owner = ring_at(far if d == 0 else -far)
+        i = ring_sem(d, g, c, s)
+        total = dot(XT[pl.ds(al(owner * TOK + c * 128, 128), 128), :], E[g])
+        if s > 1:
+            rs_copy(d, g, c, s - 1).wait_recv()
+            total = total + RB[i - 1].astype(f32)
+        SB[i] = total.astype(bf16)
+        rs_copy(d, g, c, s).start()
 
     def rs_end(g):
-        total = term(z, g)
-        for d in (0, 1):
-            rs_copy(d, g, 4).wait_recv()
-            total = total + RB[ag_sem(d, g, 4)].astype(f32)
+        total = dot(XT[pl.ds(al(z * TOK, TOK), TOK), :], E[g])
+        came = []
+        for c in (0, 1):
+            for d in (0, 1):
+                rs_copy(d, g, c, hops(d, c)).wait_recv()
+            first, second = (RB[ring_sem(d, g, c, hops(d, c))].astype(f32) for d in (0, 1))
+            came.append(first + second)
+        total = total + jnp.concatenate(came, axis=0)
         ck, cv = g * HD, 512 + g * HD
         wide_gain = GC[...]
         tk, tv = total[:, 0:HD], total[:, HD : 2 * HD]
@@ -528,7 +517,7 @@
     acts = dict(
         ag=ag_step, own=ag_own, tab=tables, inv=inverse, tr=x_transpose, pp=first_projection, po=project_own,
         gs=start_group, ge=end_group, rs=rs_step, ew=lambda g: e_copy(g).wait_recv(), re=rs_end, us=send_upstream,
-        uo=lambda j: finish(0, j, upstream(0, j)), ui=upstream_in, o=outer,
+        uo=lambda j: finish(0, j, upstream(0, j)), ui=upstream_in, o=outer, dq=query_gradient,
     )
 
     def play(items):
@@ -546,10 +535,10 @@
                 def _(items=items):
                     play(items)
 
-        head_pair(n * 2 * HD)
+        heads(n)
         return 0
 
-    lax.fori_loop(0, GROUPS * PAIRS, step, 0)
+    lax.fori_loop(0, GROUPS * 2, step, 0)
     play(AFTER)
     spread = jnp.where(eye, jnp.concatenate([GT[...], GT[...]], axis=1), 0.0)
     dg_out[...] = jnp.sum(spread, axis=0, keepdims=True)
@@ -561,10 +550,11 @@
     def drain(g, _):
         p_copy(g).wait_send()
         e_copy(g).wait_send()
-        for s in (1, 2, 3, 4):
-            for d in (0, 1):
-                ag_send(d, g, s).wait_send()
-                rs_copy(d, g, s).wait_send()
+        for d in (0, 1):
+            for c in (0, 1):
+                for s in range(1, hops(d, c) + 1):
+                    ag_send(d, g, c, s).wait_send()
+                    rs_copy(d, g, c, s).wait_send()
         return 0
 
     lax.fori_loop(0, GROUPS, drain, 0)
@@ -609,17 +599,19 @@
         v((GROUPS, 2 * TOK, 256), bf16),
         v((PIECES, TOK, PIECE), bf16),
         v((PIECES, TOK, PIECE), bf16),
-        v((32, TOK, 256), bf16),
-        v((32, TOK, 256), bf16),
-        v((TOK, HD), f32),
-        v((TOK, HD), f32),
-        v((TOK, HD), f32),
-        v((TOK, HD), f32),
-        v((128, 256), f32),
-        v((256, 256), f32),
+        v((64, 128, 256), bf16),
+        v((64, 128, 256), bf16),
+        v((TOK, HD), f32),
+        v((TOK, HD), f32),
+        v((TOK, HD), f32),
+        v((TOK, HD), f32),
+        v((128, 512), f32),
+        v((256, 512), f32),
+        v((8, 256, 512), bf16),
+        v((8, 128, 512), bf16),
         v((TOK, HD), bf16),
         v((TOK, HD), bf16),
-        v((HD, TOK), bf16),
+        v((GROUPS, HD, TOK), bf16),
         v((TOK, HD), f32),
         v((TOK, HD), f32),
         v((TOK, HD), f32),
@@ -639,7 +631,7 @@
         v((256, 128), f32),
         v((1, 256), jnp.int32),
         v((1, 256), bf16),
-        dma((32,)), dma((32,)), dma((32,)), dma((32,)),
+        dma((64,)), dma((64,)), dma((64,)), dma((64,)),
         dma((4,)), dma((4,)), dma((4,)), dma((4,)),
         dma((4,)), dma((4,)), dma((4,)), dma((4,)),
         dma((12,)), dma((12,)), dma((10,)),

time: 102 us -> 96.8 us (0.949)
  Pallas kernels: 101 us -> 95.9 us
    pallas_call x1, Pallas kernels: 98.8 us -> 93.3 us  [on_device(): pl.pallas_call(kernel, out_shape=tuple((pltpu.VMEM(a.shape, a.dtype) for...]
where the time goes in v3:
time: 96.8 us; the launch traced here: 96.7 us
  Pallas kernels  95.9 us (99%)
    pallas_call x1, Pallas kernels, on_device(): pl.pallas_call(kernel, out_shape=tuple((pltpu.VMEM(a.shape, a.dtype) for...  93.3 us
    pallas_call x1, Pallas kernels, on_device(): pl.pallas_call(store, out_shape=shapes, in_specs=[anywhere] * 7, out_spec...  2.6 us

profile of v3, /device:TPU:6, one launch (start us, length us, event | category | flops | bytes accessed | tf_op | source)
XLA Modules:
  0.0 96.7 jit_solution(3578838060058456437)
XLA Ops:
  0.6 93.3 %step.1 = (bf16[256,4096]{1,0:T(8,128)(2,1)S(1)}, bf16[256,4096]{1,0:T(8,128)(2,1)S(1)}, f32[1,256,1024]{2,1,0:T(8,128)S(1)}, f32[1,256]{1,0:T(1,128)S(1)}, f32[...) custom-call(bf16[256,4096]{1,0:T(8,128)(2,1)} %x_ref.1, bf16[256,4096]{1,0:T(8,128)(2,1)} %q_ref.1, ...), custom_call_target="tpu_custom_call" | custom-call | tf_op jit(solution)/shard_map/step/pallas_call | solution.py:648
  94.0 2.6 %store.1 = (bf16[256,4096]{1,0:T(8,128)(2,1)}, bf16[256,4096]{1,0:T(8,128)(2,1)}, f32[1,256,1024]{2,1,0:T(8,128)}, f32[1,256]{1,0:T(1,128)}, f32[64,256]{1,0:T(8...) custom-call(bf16[256,4096]{1,0:T(8,128)(2,1)S(1)} %get-tuple-element.21.refs_0_, ...), custom_call_target="tpu_custom_call" | custom-call | tf_op jit(solution)/shard_map/store/pallas_call | solution.py:659

commit v4 on v3

--- a/solution.py
+++ b/solution.py
@@ -28,6 +28,7 @@
 
 f32 = jnp.float32
 bf16 = jnp.bfloat16
+STORE_PARTS = 4
 VMEM_LIMIT = 44 * 2**20
 NT = (((1,), (1,)), ((), ()))
 
@@ -35,36 +36,35 @@
 BEFORE = (
     ("inv",), ("tab",), ("tr", 0, 0), ("tr", 0, 1), ("tr", 0, 2), ("tr", 0, 3), ("o", 1),
     ("ag", 0, 0, 0, 1), ("ag", 1, 0, 1, 1), ("ag", 0, 0, 1, 1), ("ag", 1, 0, 0, 1), ("o", 2),
-    ("ag", 0, 1, 0, 1), ("ag", 1, 1, 1, 1), ("tr", 1, 0), ("ag", 0, 1, 1, 1), ("ag", 1, 1, 0, 1),
-    ("ag", 0, 0, 0, 2), ("ag", 1, 0, 1, 2), ("ag", 0, 0, 1, 2), ("ag", 1, 0, 0, 2), ("o", 3),
-    ("ag", 0, 1, 0, 2), ("ag", 1, 1, 1, 2), ("own", 2), ("tr", 1, 1), ("ag", 0, 1, 1, 2),
-    ("ag", 1, 1, 0, 2), ("ag", 0, 0, 0, 3), ("ag", 1, 0, 1, 3), ("ag", 0, 0, 1, 3), ("ag", 1, 0, 0, 3),
-    ("ag", 0, 1, 0, 3), ("ag", 1, 1, 1, 3), ("own", 3), ("tr", 1, 2), ("ag", 0, 2, 0, 1),
-    ("ag", 1, 2, 1, 1), ("ag", 0, 2, 1, 1), ("ag", 1, 2, 0, 1), ("ag", 0, 1, 1, 3), ("ag", 1, 1, 0, 3),
-    ("ag", 0, 0, 0, 4), ("ag", 1, 0, 1, 4), ("po", 0), ("pp", 0), ("ag", 0, 1, 0, 4),
-    ("ag", 1, 1, 1, 4), ("pp", 1), ("po", 1), ("tr", 1, 3), ("o", 4), ("ag", 0, 3, 0, 1),
-    ("ag", 1, 3, 1, 1), ("ag", 0, 3, 1, 1), ("ag", 1, 3, 0, 1), ("ag", 0, 2, 0, 2), ("ag", 1, 2, 1, 2),
+    ("ag", 0, 1, 0, 1), ("ag", 1, 1, 1, 1), ("ag", 0, 1, 1, 1), ("ag", 1, 1, 0, 1), ("tr", 1, 0),
+    ("ag", 0, 0, 0, 2), ("ag", 1, 0, 1, 2), ("ag", 0, 0, 1, 2), ("ag", 1, 0, 0, 2), ("ag", 0, 1, 0, 2),
+    ("ag", 1, 1, 1, 2), ("own", 2), ("o", 3), ("ag", 0, 1, 1, 2), ("ag", 1, 1, 0, 2), ("tr", 1, 1),
+    ("ag", 0, 0, 0, 3), ("ag", 1, 0, 1, 3), ("ag", 0, 0, 1, 3), ("ag", 1, 0, 0, 3), ("ag", 0, 1, 0, 3),
+    ("ag", 1, 1, 1, 3), ("own", 3), ("ag", 0, 2, 0, 1), ("ag", 1, 2, 1, 1), ("tr", 1, 2),
+    ("ag", 0, 2, 1, 1), ("ag", 1, 2, 0, 1), ("ag", 0, 1, 1, 3), ("ag", 1, 1, 0, 3), ("ag", 0, 0, 0, 4),
+    ("ag", 1, 0, 1, 4), ("po", 0), ("ag", 0, 1, 0, 4), ("ag", 1, 1, 1, 4), ("po", 1), ("pp", 0),
+    ("pp", 1), ("tr", 1, 3), ("ag", 0, 3, 0, 1), ("ag", 1, 3, 1, 1), ("o", 4), ("ag", 0, 3, 1, 1),
+    ("ag", 1, 3, 0, 1), ("ag", 0, 2, 0, 2), ("ag", 1, 2, 1, 2), ("ag", 0, 2, 1, 2), ("ag", 1, 2, 0, 2),
     ("gs", 0),
 )
 DURING = (
     (),
+    (),
     (
-        ("ag", 0, 2, 1, 2), ("ag", 1, 2, 0, 2),
+        ("ag", 0, 3, 0, 2), ("ag", 1, 3, 1, 2), ("ge", 0), ("dq", 0), ("ag", 0, 3, 1, 2),
+        ("ag", 1, 3, 0, 2), ("gs", 1),
     ),
     (
-        ("ag", 0, 3, 0, 2), ("ag", 1, 3, 1, 2), ("ge", 0), ("dq", 0), ("gs", 1), ("ag", 0, 3, 1, 2),
-        ("ag", 1, 3, 0, 2),
+        ("ag", 0, 2, 0, 3), ("ag", 1, 2, 1, 3),
     ),
-    (),
     (
-        ("ag", 0, 2, 0, 3), ("ag", 1, 2, 1, 3), ("ge", 1), ("dq", 1), ("ag", 0, 2, 1, 3),
-        ("ag", 1, 2, 0, 3), ("dq", 2), ("dq", 3), ("o", 5), ("ag", 0, 3, 0, 3), ("ag", 1, 3, 1, 3),
-        ("ew", 0), ("rs", 0, 0, 1, 1), ("rs", 1, 0, 0, 1), ("rs", 0, 0, 0, 1), ("rs", 1, 0, 1, 1),
-        ("ag", 0, 3, 1, 3), ("ag", 1, 3, 0, 3), ("ag", 0, 2, 0, 4), ("ag", 1, 2, 1, 4), ("pp", 2),
-        ("po", 2), ("ew", 1), ("rs", 0, 1, 1, 1), ("rs", 1, 1, 0, 1), ("rs", 0, 1, 0, 1),
-        ("rs", 1, 1, 1, 1), ("ag", 0, 3, 0, 4), ("ag", 1, 3, 1, 4), ("pp", 3), ("po", 3),
-        ("rs", 0, 0, 1, 2), ("rs", 1, 0, 0, 2), ("o", 6), ("rs", 0, 0, 0, 2), ("rs", 1, 0, 1, 2),
-        ("gs", 2), ("rs", 0, 1, 1, 2), ("rs", 1, 1, 0, 2),
+        ("ag", 0, 2, 1, 3), ("ag", 1, 2, 0, 3), ("ge", 1), ("dq", 1), ("dq", 2), ("ag", 0, 3, 0, 3),
+        ("ag", 1, 3, 1, 3), ("dq", 3), ("ew", 0), ("rs", 0, 0, 1, 1), ("rs", 1, 0, 0, 1),
+        ("rs", 0, 0, 0, 1), ("rs", 1, 0, 1, 1), ("o", 5), ("ag", 0, 3, 1, 3), ("ag", 1, 3, 0, 3),
+        ("ag", 0, 2, 0, 4), ("ag", 1, 2, 1, 4), ("pp", 2), ("po", 2), ("ew", 1), ("rs", 0, 1, 1, 1),
+        ("rs", 1, 1, 0, 1), ("ag", 0, 3, 0, 4), ("ag", 1, 3, 1, 4), ("rs", 0, 1, 0, 1), ("rs", 1, 1, 1, 1),
+        ("pp", 3), ("po", 3), ("rs", 0, 0, 1, 2), ("rs", 1, 0, 0, 2), ("rs", 0, 0, 0, 2),
+        ("rs", 1, 0, 1, 2), ("o", 6), ("gs", 2), ("rs", 0, 1, 1, 2), ("rs", 1, 1, 0, 2),
     ),
     (),
     (
@@ -81,11 +81,11 @@
     ("rs", 0, 3, 1, 1), ("rs", 1, 3, 0, 1), ("rs", 0, 3, 0, 1), ("rs", 1, 3, 1, 1), ("us", 1),
     ("us", 2), ("us", 3), ("rs", 0, 1, 0, 4), ("rs", 1, 1, 1, 4), ("o", 7), ("rs", 0, 2, 1, 2),
     ("rs", 1, 2, 0, 2), ("rs", 0, 2, 0, 2), ("rs", 1, 2, 1, 2), ("re", 0), ("rs", 0, 3, 1, 2),
-    ("rs", 1, 3, 0, 2), ("ui", 0), ("rs", 0, 3, 0, 2), ("rs", 1, 3, 1, 2), ("re", 1),
-    ("rs", 0, 2, 1, 3), ("rs", 1, 2, 0, 3), ("rs", 0, 2, 0, 3), ("rs", 1, 2, 1, 3), ("ui", 1),
+    ("rs", 1, 3, 0, 2), ("ui", 0), ("dr", 0), ("rs", 0, 3, 0, 2), ("rs", 1, 3, 1, 2), ("re", 1),
+    ("rs", 0, 2, 1, 3), ("rs", 1, 2, 0, 3), ("rs", 0, 2, 0, 3), ("rs", 1, 2, 1, 3), ("ui", 1), ("dr", 1),
     ("rs", 0, 3, 1, 3), ("rs", 1, 3, 0, 3), ("rs", 0, 3, 0, 3), ("rs", 1, 3, 1, 3), ("rs", 0, 2, 0, 4),
     ("rs", 1, 2, 1, 4), ("ui", 2), ("rs", 0, 3, 0, 4), ("rs", 1, 3, 1, 4), ("re", 2), ("ui", 3),
-    ("re", 3),
+    ("dr", 2), ("re", 3),
 )
 
 
@@ -141,9 +141,8 @@
     ld_m1 = pltpu.make_async_copy(fmo_ref, M01.at[64:128], l_s.at[7])
     ld_doc = pltpu.make_async_copy(doc_ref, DOC, l_s.at[8])
     ld_gain = pltpu.make_async_copy(gain_ref, GAIN, l_s.at[9])
-    for c in (ld_w, ld_gain, ld_x, ld_xo, ld_f, ld_m0, ld_m1, ld_doc, ld_q, ld_do):
-        c.start()
-
+    ld_gain.start()
+    ld_w.start()
     barrier = pltpu.get_barrier_semaphore()
     for d in (left, right, partner, sibling, across, *xpeer):
         pl.semaphore_signal(barrier, inc=1, device_id=d, device_id_type=pl.DeviceIdType.MESH)
@@ -206,11 +205,13 @@
 
     scale_w(0)
     pl.semaphore_wait(barrier, 8)
+    ag_own(0)
     for j in range(PIECES):
         x_copy(j).start()
-    ag_own(0)
     scale_w(1)
     ag_own(1)
+    for c in (ld_x, ld_xo, ld_f, ld_m0, ld_m1, ld_doc, ld_q, ld_do):
+        c.start()
     scale_w(2)
     scale_w(3)
 
@@ -514,10 +515,44 @@
         u_copy(j).wait_recv()
         finish(1, j, UIN[j].astype(f32))
 
+    def drain_ring(copy, g):
+        for d in (0, 1):
+            for c in (0, 1):
+                for s in range(1, hops(d, c) + 1):
+                    copy(d, g, c, s).wait_send()
+
+    def drain(k):
+        if k == 0:
+            for j in range(PIECES):
+                x_copy(j).wait_send()
+
+            def gathers(g, _):
+                p_copy(g).wait_send()
+                drain_ring(ag_send, g)
+                return 0
+
+            lax.fori_loop(0, GROUPS, gathers, 0)
+        elif k == 1:
+
+            def sums(g, _):
+                drain_ring(rs_copy, g)
+                return 0
+
+            lax.fori_loop(0, 2, sums, 0)
+            for g in range(GROUPS):
+                e_copy(g).wait_send()
+            for c in (o_frag, o_state, o_y, o_pack, o_back_y, o_back_s):
+                c.wait_send()
+            for j in range(3):
+                o_x(j).wait_send()
+                o_back_x(j).wait_send()
+        else:
+            drain_ring(rs_copy, 2)
+
     acts = dict(
         ag=ag_step, own=ag_own, tab=tables, inv=inverse, tr=x_transpose, pp=first_projection, po=project_own,
         gs=start_group, ge=end_group, rs=rs_step, ew=lambda g: e_copy(g).wait_recv(), re=rs_end, us=send_upstream,
-        uo=lambda j: finish(0, j, upstream(0, j)), ui=upstream_in, o=outer, dq=query_gradient,
+        uo=lambda j: finish(0, j, upstream(0, j)), ui=upstream_in, o=outer, dq=query_gradient, dr=drain,
     )
 
     def play(items):
@@ -543,32 +578,23 @@
     spread = jnp.where(eye, jnp.concatenate([GT[...], GT[...]], axis=1), 0.0)
     dg_out[...] = jnp.sum(spread, axis=0, keepdims=True)
 
+    drain_ring(rs_copy, 3)
     for j in range(PIECES):
-        x_copy(j).wait_send()
         u_copy(j).wait_send()
-
-    def drain(g, _):
-        p_copy(g).wait_send()
-        e_copy(g).wait_send()
-        for d in (0, 1):
-            for c in (0, 1):
-                for s in range(1, hops(d, c) + 1):
-                    ag_send(d, g, c, s).wait_send()
-                    rs_copy(d, g, c, s).wait_send()
-        return 0
-
-    lax.fori_loop(0, GROUPS, drain, 0)
-    for c in (o_frag, o_state, o_y, o_pack, o_back_y, o_back_s):
-        c.wait_send()
-    for j in range(3):
-        o_x(j).wait_send()
-        o_back_x(j).wait_send()
 
 
 def store(*refs):
     n = len(refs) // 2
     sems = refs[-1]
-    copies = [pltpu.make_async_copy(refs[i], refs[n + i], sems.at[i]) for i in range(n)]
+    copies = []
+    for src, dst in zip(refs[:n], refs[n : 2 * n]):
+        parts = STORE_PARTS if math.prod(src.shape) >= 2**18 else 1
+        rows = src.shape[-2] // parts
+        for i in range(parts):
+            at = (slice(i * rows, (i + 1) * rows),) if parts > 1 else ()
+            at = (0, *at) if parts > 1 and len(src.shape) == 3 else at
+            a, b = (src.at[at], dst.at[at]) if at else (src, dst)
+            copies.append(pltpu.make_async_copy(a, b, sems.at[len(copies)]))
     for c in copies:
         c.start()
     for c in copies:
@@ -661,7 +687,7 @@
         out_shape=shapes,
         in_specs=[anywhere] * 7,
         out_specs=(hbm,) * 7,
-        scratch_shapes=[dma((7,))],
+        scratch_shapes=[dma((3 + 4 * STORE_PARTS,))],
         compiler_params=pltpu.CompilerParams(vmem_limit_bytes=2**20),
         name="store",
     )(*results)

time: 96.8 us -> 96.6 us (level)
  no operation moved by 1% of the time
where the time goes in v4:
time: 96.6 us; the launch traced here: 96.5 us
  Pallas kernels  95.7 us (99%)
    pallas_call x1, Pallas kernels, on_device(): pl.pallas_call(kernel, out_shape=tuple((pltpu.VMEM(a.shape, a.dtype) for...  93 us
    pallas_call x1, Pallas kernels, on_device(): pl.pallas_call(store, out_shape=shapes, in_specs=[anywhere] * 7, out_spec...  2.68 us

profile of v4, /device:TPU:6, one launch (start us, length us, event | category | flops | bytes accessed | tf_op | source)
XLA Modules:
  0.0 96.5 jit_solution(3242314524061549969)
XLA Ops:
  0.6 93.0 %step.1 = (bf16[256,4096]{1,0:T(8,128)(2,1)S(1)}, bf16[256,4096]{1,0:T(8,128)(2,1)S(1)}, f32[1,256,1024]{2,1,0:T(8,128)S(1)}, f32[1,256]{1,0:T(1,128)S(1)}, f32[...) custom-call(bf16[256,4096]{1,0:T(8,128)(2,1)} %x_ref.1, bf16[256,4096]{1,0:T(8,128)(2,1)} %q_ref.1, ...), custom_call_target="tpu_custom_call" | custom-call | tf_op jit(solution)/shard_map/step/pallas_call | solution.py:674
  93.6 2.7 %store.1 = (bf16[256,4096]{1,0:T(8,128)(2,1)}, bf16[256,4096]{1,0:T(8,128)(2,1)}, f32[1,256,1024]{2,1,0:T(8,128)}, f32[1,256]{1,0:T(1,128)}, f32[64,256]{1,0:T(8...) custom-call(bf16[256,4096]{1,0:T(8,128)(2,1)S(1)} %get-tuple-element.21.refs_0_, ...), custom_call_target="tpu_custom_call" | custom-call | tf_op jit(solution)/shard_map/store/pallas_call | solution.py:685
